TPU v7x, 32 devices: a whole 2x2x4 slice. The times are simulated.
32 devices in a mesh: seq: 4 (over z), chan: 8 (over y, x, core).
Axes of the slice: x: 2, y: 2, z: 4, core: 2. Of those that a mesh axis runs over, the one named last changes fastest.
Arguments:
- tokens: bfloat16 [8192, 768], P(('seq', 'chan')), may hold values from -6 to 6
- resets: int32 [8192], P('seq'), may hold values 0 or 1
- cotangent: bfloat16 [8192, 768], P(('seq', 'chan')), may hold values from -6 to 6
- norm_gain: float32 [768], replicated, may hold values from 0.5 to 1.5
- in_weight: float32 [2, 768, 1536], P(None, None, 'chan'), may hold values from -0.21875 to 0.21875
- x_weight: float32 [1536, 80], P('chan'), may hold values from -0.15625 to 0.15625
- dt_weight: float32 [48, 1536], P(None, 'chan'), may hold values from -1.5 to 1.5
- out_weight: float32 [1536, 768], P('chan'), may hold values from -0.375 to 0.375
- chan_params: float32 [23, 1536], P(None, 'chan'), may hold values from -7 to 3, as said below
- gain_first: float32 [768], replicated, may hold values from -56 to 56
- gain_second: float32 [768], replicated, may hold values from 3.2768 to 52.4288
- in_first: float32 [2, 768, 1536], P(None, None, 'chan'), may hold values from -28 to 28
- in_second: float32 [2, 768, 1536], P(None, None, 'chan'), may hold values from 0.8192 to 13.1072
- x_first: float32 [1536, 80], P('chan'), may hold values from -320 to 320
- x_second: float32 [1536, 80], P('chan'), may hold values from 102.4 to 1638.4
- dt_first: float32 [48, 1536], P(None, 'chan'), may hold values from -32 to 32
- dt_second: float32 [48, 1536], P(None, 'chan'), may hold values from 1.024 to 16.384
- out_first: float32 [1536, 768], P('chan'), may hold values from -24 to 24
- out_second: float32 [1536, 768], P('chan'), may hold values from 0.65536 to 10.6496
- chan_first: float32 [23, 1536], P(None, 'chan'), may hold values from -32 to 32
- chan_second: float32 [23, 1536], P(None, 'chan'), may hold values from 1.024 to 16.384
Outputs:
- mixed: bfloat16 [8192, 768], P(('seq', 'chan'))
- tokens_grad: float32 [8192, 768], P(('seq', 'chan'))
- gain_master: float32 [768], replicated
- gain_first_out: float32 [768], replicated
- gain_second_out: float32 [768], replicated
- gain_copy: bfloat16 [768], replicated
- in_master: float32 [2, 768, 1536], P(None, None, 'chan')
- in_first_out: float32 [2, 768, 1536], P(None, None, 'chan')
- in_second_out: float32 [2, 768, 1536], P(None, None, 'chan')
- in_copy: bfloat16 [2, 768, 1536], P(None, None, 'chan')
- x_master: float32 [1536, 80], P('chan')
- x_first_out: float32 [1536, 80], P('chan')
- x_second_out: float32 [1536, 80], P('chan')
- x_copy: bfloat16 [1536, 80], P('chan')
- dt_master: float32 [48, 1536], P(None, 'chan')
- dt_first_out: float32 [48, 1536], P(None, 'chan')
- dt_second_out: float32 [48, 1536], P(None, 'chan')
- dt_copy: bfloat16 [48, 1536], P(None, 'chan')
- out_master: float32 [1536, 768], P('chan')
- out_first_out: float32 [1536, 768], P('chan')
- out_second_out: float32 [1536, 768], P('chan')
- out_copy: bfloat16 [1536, 768], P('chan')
- chan_master: float32 [23, 1536], P(None, 'chan')
- chan_first_out: float32 [23, 1536], P(None, 'chan')
- chan_second_out: float32 [23, 1536], P(None, 'chan')
- chan_copy: bfloat16 [23, 1536], P(None, 'chan')
Inputs may be any that keep to these rules, and one draw needn't show every extreme that they name: `resets`: 1 marks the first token of a document; every packed row of 2048 tokens starts one as well. `chan_params`: the step bias row holds softplus inverses of steps between 0.001 and 0.1.
All inputs are finite; a program needn't handle non-finite values. No bound on the sum of `resets` on one device may be relied on, other than what follows from the above.
Results may differ from a plain program's by a relative error of at most 0.018.
Values may be sent and summed in bfloat16 or wider, within the bound.
A program may use at most 448 MiB of HBM per device.

v0:
```python
import functools

import jax
import jax.numpy as jnp
from jax import lax
from jax.experimental import pallas as pl
from jax.experimental.pallas import tpu as pltpu
from jax.sharding import PartitionSpec as P

DS = 16
DR = 48
KC = 4
SEQ_LEN = 2048
STEP = 10
SLABS = 16
LANES = 128
NG = 16
CT = 2
SEGMENTS = 4
PIECES = 4
MIB = 1024 * 1024
MESH = pl.DeviceIdType.MESH

highest = lax.Precision.HIGHEST
norm_epsilon = 1e-05
beta_first = 0.9
beta_second = 0.999
adam_epsilon = 1e-08
weight_decay = 0.1
rate_gain = 0.4
rate_inner = 0.05
rate_project = 0.04
rate_step = 0.1
rate_output = 0.08
rate_channel = 0.5
LOG2E = 1.4426950408889634
LN2 = 0.6931471805599453
HUGE = 1e30
f32 = jnp.float32
bf16 = jnp.bfloat16


def adamw_core(master, moment_one, moment_two, gradient, rate_value):
    first_new = beta_first * moment_one + (1.0 - beta_first) * gradient
    second_new = beta_second * moment_two + (1.0 - beta_second) * gradient * gradient
    scale = jnp.sqrt(second_new * (1.0 / (1.0 - beta_second**STEP))) + adam_epsilon
    corrected = first_new * (rate_value / (1.0 - beta_first**STEP)) / scale
    master_new = master * (1.0 - rate_value * weight_decay) - corrected
    return (master_new, first_new, second_new)


def dot_nn(a, b, precision=None):
    return lax.dot_general(a, b, (((1,), (0,)), ((), ())), precision=precision, preferred_element_type=f32)


def dot_nt(a, b, precision=None):
    return lax.dot_general(a, b, (((1,), (1,)), ((), ())), precision=precision, preferred_element_type=f32)


def dot_tn(a, b, precision=None):
    return lax.dot_general(a, b, (((0,), (0,)), ((), ())), precision=precision, preferred_element_type=f32)


def slab(s):
    return slice(s * LANES, (s + 1) * LANES)


def flip(index, bits):
    result = index
    place = 1
    while place <= bits:
        if bits & place:
            result = result + place * (1 - 2 * ((index // place) % 2))
        place *= 2
    return result


class Here:
    def __init__(self, chan_size):
        self.seq = lax.axis_index("seq")
        self.chan = lax.axis_index("chan")
        self.chips = chan_size // 2
        self.core = self.chan % 2
        self.chip = self.chan // 2
        self.partner = self.chan + 1 - 2 * self.core

    def same_core(self, k):
        return flip(self.chip, k) * 2 + self.core

    def other_core(self, k):
        return flip(self.chip, k) * 2 + 1 - self.core

    def copy(self, src, dst, send, recv, chan):
        return pltpu.make_async_remote_copy(
            src_ref=src, dst_ref=dst, send_sem=send, recv_sem=recv,
            device_id=(self.seq, chan), device_id_type=MESH,
        )


class Gather:
    def __init__(self, here, buf, hop, send, recv, rsend, rrecv, fsend, frecv):
        self.here, self.buf, self.hop = here, buf, hop
        self.send, self.recv, self.rsend, self.rrecv = send, recv, rsend, rrecv
        self.fsend, self.frecv = fsend, frecv
        self.half = PIECES // 2

    def place(self, j, q):
        per_row = self.buf.shape[2]
        step = SLABS // PIECES
        return self.buf.at[j // per_row, pl.ds(q * step, step), j % per_row]

    def direct(self, k, q, shard):
        h = self.here
        to = h.partner if k == 0 else h.same_core(k)
        return h.copy(self.place(shard, q), self.place(shard, q), self.send.at[k, q], self.recv.at[k, q], to)

    def relay(self, k, q, shard):
        return self.here.copy(
            self.place(shard, q), self.place(shard, q), self.rsend.at[k, q], self.rrecv.at[k, q], self.here.partner
        )

    def onward(self, q, shard, k):
        return self.here.copy(
            self.place(shard, q), self.place(shard, q), self.fsend.at[q], self.frecv.at[q], self.here.same_core(k)
        )

    def pieces(self, k):
        every = list(range(PIECES))
        return every[self.half :] + every[: self.half] if k == 1 else every

    def start(self):
        h = self.here
        for i in range(PIECES):
            for k in range(1, 3 if self.hop else h.chips):
                self.direct(k, self.pieces(k)[i] if self.hop else i, h.chan).start()
        for q in range(PIECES):
            self.direct(0, q, h.chan).start()

    def take(self, k, q):
        shard = self.here.same_core(k)
        self.direct(k, q, shard).wait_recv()
        if self.hop and (q >= self.half) == (k == 1):
            self.onward(q, shard, 3 - k).start()
        self.relay(k, q, shard).start()

    def take_across(self, q):
        shard = self.here.same_core(3)
        self.onward(q, shard, 1).wait_recv()
        self.relay(3, q, shard).start()

    def pass_on(self, i):
        if not self.hop:
            if i < PIECES:
                for k in range(1, self.here.chips):
                    self.take(k, i)
        elif i < PIECES:
            self.take(1, self.pieces(1)[i])
            self.take(2, self.pieces(2)[i])
        else:
            for q in range(self.half):
                self.take_across(q)
                self.take_across(self.half + q)

    def arrive(self, q):
        self.direct(0, q, self.here.partner).wait_recv()
        for k in range(1, self.here.chips):
            self.relay(k, q, self.here.other_core(k)).wait_recv()

    def close(self):
        for q in range(PIECES):
            for k in range(3 if self.hop else self.here.chips):
                self.direct(k, q, self.here.chan).wait_send()
            if self.hop:
                k = 1 if q >= self.half else 2
                self.onward(q, self.here.same_core(k), 3 - k).wait_send()
            for k in range(1, self.here.chips):
                self.relay(k, q, self.here.same_core(k)).wait_send()


class Reduce:
    def __init__(self, here, part, from_pair, pair, from_chips, total, send, recv):
        self.here, self.part, self.from_pair, self.pair = here, part, from_pair, pair
        self.from_chips, self.total, self.send, self.recv = from_chips, total, send, recv
        self.half = part.shape[1] // 2
        self.own = self.half // here.chips

    def half_cols(self, core):
        return pl.ds(pl.multiple_of(core * self.half, LANES), self.half)

    def own_cols(self, chip):
        return pl.ds(pl.multiple_of(chip * self.own, LANES), self.own)

    def own_total(self, chip):
        start = pl.multiple_of(self.here.core * self.half + chip * self.own, LANES)
        return self.total.at[:, pl.ds(start, self.own)]

    def swap(self):
        h = self.here
        return h.copy(
            self.part.at[:, self.half_cols(1 - h.core)], self.from_pair, self.send.at[0], self.recv.at[0], h.partner
        )

    def scatter(self, k):
        h = self.here
        return h.copy(
            self.pair.at[:, self.own_cols(flip(h.chip, k))], self.from_chips.at[k - 1],
            self.send.at[k], self.recv.at[k], h.same_core(k),
        )

    def spread(self, k, chip):
        h = self.here
        index = h.chips + k
        return h.copy(
            self.own_total(chip), self.own_total(chip), self.send.at[index], self.recv.at[index], h.same_core(k)
        )

    def share(self, core):
        h = self.here
        cols = self.total.at[:, self.half_cols(core)]
        return h.copy(cols, cols, self.send.at[h.chips], self.recv.at[h.chips], h.partner)

    def step1(self):
        self.swap().start()

    def step2(self):
        self.swap().wait()
        pair = self.part[:, self.half_cols(self.here.core)].astype(f32) + self.from_pair[...].astype(f32)
        self.from_pair[...] = pair.astype(self.from_pair.dtype)
        self.pair[...] = pair.astype(bf16)
        for k in range(1, self.here.chips):
            self.scatter(k).start()

    def step3(self):
        total = self.from_pair[:, self.own_cols(self.here.chip)].astype(f32)
        for k in range(1, self.here.chips):
            self.scatter(k).wait_recv()
            total = total + self.from_chips[k - 1].astype(f32)
        start = pl.multiple_of(self.here.core * self.half + self.here.chip * self.own, LANES)
        self.total[:, pl.ds(start, self.own)] = total.astype(bf16)
        for k in range(1, self.here.chips):
            self.spread(k, self.here.chip).start()

    def step4(self):
        for k in range(1, self.here.chips):
            self.spread(k, flip(self.here.chip, k)).wait_recv()
        self.share(self.here.core).start()

    def step5(self):
        self.share(1 - self.here.core).wait_recv()

    def close(self):
        for k in range(1, self.here.chips):
            self.scatter(k).wait_send()
            self.spread(k, self.here.chip).wait_send()
        self.share(self.here.core).wait_send()


def reorder(own_rows):
    lanes = own_rows // SLABS
    r = lax.broadcasted_iota(jnp.int32, (own_rows, own_rows), 0)
    q = lax.broadcasted_iota(jnp.int32, (own_rows, own_rows), 1)
    return jnp.where(q == (r % lanes) * SLABS + r // lanes, 1.0, 0.0)


class Scatter:
    def __init__(self, here, part, pair, landed, send1, recv1, send2, recv2):
        self.here, self.part, self.pair, self.landed = here, part, pair, landed
        self.send1, self.recv1, self.send2, self.recv2 = send1, recv1, send2, recv2
        self.slots, self.rows, self.per_row = part.shape[0], pair.shape[0], pair.shape[2]

    def slabs(self, q):
        step = SLABS // PIECES
        return pl.ds(q * step, step)

    def swap(self, r, q):
        h = self.here
        index = r * PIECES + q
        return h.copy(
            self.part.at[r % self.slots, self.slabs(q), :, 1 - h.core], self.pair.at[r, self.slabs(q)],
            self.send1.at[index], self.recv1.at[index], h.partner,
        )

    def out(self, k, q):
        h = self.here
        chip = flip(h.chip, k)
        index = (k - 1) * PIECES + q
        return h.copy(
            self.pair.at[chip // self.per_row, self.slabs(q), chip % self.per_row],
            self.landed.at[k - 1, self.slabs(q)],
            self.send2.at[index], self.recv2.at[index], h.same_core(k),
        )

    def add(self, r, q):
        step = SLABS // PIECES
        self.swap(r, q).wait()
        for s in range(q * step, (q + 1) * step):
            mine = self.part[r % self.slots, s, :, self.here.core].astype(f32)
            self.pair[r, s] = (self.pair[r, s].astype(f32) + mine).astype(bf16)

    def produce(self, partial, pipelined, between):
        step = SLABS // PIECES
        _, _, per_row, _, lanes, width = self.part.shape
        for r in range(self.rows):
            for q in range(PIECES):
                start = (r * SLABS + q * step) * LANES
                rows = partial(slice(start, start + step * LANES)).astype(bf16)
                self.part[r % self.slots, q * step : (q + 1) * step] = rows.reshape(step, per_row, 2, lanes, width)
                self.swap(r, q).start()
                if pipelined and r + 1 == self.rows and q > 0:
                    self.send(q - 1)
                    if q == 1:
                        between()
            if r + 1 < self.rows:
                for q in range(PIECES):
                    self.add(r, q)

    def send(self, q):
        self.add(self.rows - 1, q)
        for k in range(1, self.here.chips):
            self.out(k, q).start()

    def finish(self, result):
        h = self.here
        lanes = self.part.shape[4]
        for q in range(PIECES):
            for k in range(1, h.chips):
                self.out(k, q).wait()
        for s in range(SLABS):
            total = self.pair[h.chip // self.per_row, s, h.chip % self.per_row].astype(f32)
            for k in range(1, h.chips):
                total = total + self.landed[k - 1, s].astype(f32)
            result[s * lanes : (s + 1) * lanes, :] = total


class SeqSum:
    def __init__(self, here, seq_size, buf, half_in, send, recv):
        self.here, self.size, self.buf, self.half_in = here, seq_size, buf, half_in
        self.send, self.recv = send, recv
        self.half = buf.shape[0] // 2
        self.levels = seq_size.bit_length() - 1

    def rows(self, side):
        return pl.ds(pl.multiple_of(side * self.half, 16), self.half)

    def copy(self, index, src, dst, bit):
        h = self.here
        return pltpu.make_async_remote_copy(
            src_ref=src, dst_ref=dst, send_sem=self.send.at[index], recv_sem=self.recv.at[index],
            device_id=(flip(h.seq, bit), h.chan), device_id_type=MESH,
        )

    def level(self, i):
        side = self.here.seq % 2
        rows = self.rows(1 - side) if i == 0 else self.rows(side)
        return self.copy(i, self.buf.at[rows], self.half_in.at[i], 1 << i)

    def back(self):
        return self.copy(self.levels, self.buf.at[self.rows(self.here.seq % 2)], self.half_in.at[self.levels], 1)

    def start(self):
        self.level(0).start()

    def step(self, i):
        side = self.here.seq % 2
        self.level(i).wait()
        rows = self.rows(side)
        total = self.buf[rows, :].astype(f32) + self.half_in[i].astype(f32)
        self.buf[rows, :] = total.astype(bf16)
        if i + 1 < self.levels:
            self.level(i + 1).start()
        else:
            self.back().start()

    def finish(self, out, sems):
        side = self.here.seq % 2
        self.back().wait()
        copies = [
            pltpu.make_async_copy(self.buf.at[self.rows(side)], out.at[self.rows(side)], sems.at[0]),
            pltpu.make_async_copy(self.half_in.at[self.levels], out.at[self.rows(1 - side)], sems.at[1]),
        ]
        for c in copies:
            c.start()
        return copies


def iota(shape, dim):
    return lax.broadcasted_iota(jnp.int32, shape, dim)


def row_masks(resets_ref, mask_ref):
    per_row = SEQ_LEN // LANES
    chunk, place = iota((SLABS, LANES), 1), iota((SLABS, LANES), 0)
    group = LANES // SLABS
    pick_row = jnp.where(iota((LANES, per_row), 0) // group == iota((LANES, per_row), 1), 1.0, 0.0).astype(bf16)
    pick_place = jnp.where(iota((SLABS, LANES), 1) % SLABS == iota((SLABS, LANES), 0), 1.0, 0.0).astype(bf16)
    own_chunk = iota((LANES, LANES), 1) // SLABS == iota((LANES, LANES), 0) % group

    def before(values):
        moved = pltpu.roll(values, 1, 0)
        return jnp.where(place == 0, pltpu.roll(moved, 1, 1), moved)

    for r in range(mask_ref.shape[1] // SEQ_LEN):
        block = resets_ref[r * per_row : (r + 1) * per_row, :].astype(f32).astype(bf16)
        spread = jnp.where(own_chunk, dot_nn(pick_row, block), 0.0).astype(bf16)
        start = dot_nt(pick_place, spread)
        start = jnp.where((place == 0) & (chunk == 0), 1.0, start)
        keep1 = 1.0 - start
        keep2 = keep1 * before(keep1)
        keep3 = keep2 * before(before(keep1))
        for s in range(SLABS):
            cols = slice(r * SEQ_LEN + s * LANES, r * SEQ_LEN + (s + 1) * LANES)
            for j, values in enumerate((start, keep1, keep2, keep3)):
                mask_ref[j : j + 1, cols] = values[s : s + 1, :]


DECAY_COL = 8
DT_COL = 64


def softplus(values):
    e = jnp.exp(-jnp.abs(values))
    return jnp.maximum(values, 0.0) + jnp.where(e < 1e-3, e * (1.0 - e * (0.5 - e * (1.0 / 3.0))), jnp.log(1.0 + e))


def tall(channels):
    return 48 if channels % 48 == 0 else 16


def windows(total_ref, window_ref, later):
    channels = total_ref.shape[0]
    part = 96 if channels % 96 == 0 else channels
    for start in range(0, channels, part):
        rows = slice(start, start + part)
        total = total_ref[rows, :]
        for k in range(7):
            window_ref[k, rows, :] = total
            if k < 6:
                total = total + pltpu.roll(total, LANES - (1 << k) if later else 1 << k, 1)


def expand_matrix():
    return jnp.where(iota((DS * 8, DS), 0) // 8 == iota((DS * 8, DS), 1), 1.0, 0.0)


class Tiles:
    def __init__(self, channels, rows_n):
        self.rows_n, self.span = rows_n, CT * 8
        self.tiles, self.groups = channels // self.span, DS // NG
        self.per_row = self.tiles * self.groups
        self.count = rows_n * self.per_row

    def split(self, index):
        r, j = (0, index) if self.rows_n == 1 else (index // self.per_row, index % self.per_row)
        return r, j, j // self.groups, j % self.groups

    def rows(self, i):
        return pl.ds(pl.multiple_of(i * self.span, self.span), self.span)

    def cols(self, r, s):
        if self.rows_n == 1:
            return slab(s)
        return pl.ds(pl.multiple_of(r * SEQ_LEN + s * LANES, LANES), LANES)

    def loop(self, segment, body):
        lo, hi = (self.count * k // SEGMENTS for k in (segment, segment + 1))
        lax.fori_loop(lo, hi, body, 0)


def front_kernel(
    chan_size,
    tok_ref, cot_ref, gain_ref, inw_ref, xw_ref, outw_ref, ch_ref, dtw_ref, resets_ref,
    x_out, act_out, step_out, dy_out, gated_out, dgate_out, pj_out, ng_out, cg_out, h0_out, dec_out, mask_out, ct_out,
    ng, cg, xs, gs, slope, acts, dgs, wxg, part, from_pair, pair, from_chips, pj,
    mask, table, rowf, padded, step_ref, du_ref, y_ref, sums, wf, b8, c8, decb, h0, a_scr, gated, dgate,
    ag_send, ag_recv, ag_rsend, ag_rrecv, ag_fsend, ag_frecv, rd_send, rd_recv, out_sem,
):
    here = Here(chan_size)
    chips = here.chips
    own_rows, width = tok_ref.shape
    lanes = own_rows // SLABS
    rows_n, _, per_row = ng.shape[:3]
    channels, tokens = xs.shape
    t = Tiles(channels, rows_n)
    copies = []

    def save(src, dst):
        c = pltpu.make_async_copy(src, dst, out_sem.at[len(copies)])
        c.start()
        copies.append(c)

    barrier = pltpu.get_barrier_semaphore()
    for k in range(1, chips):
        pl.semaphore_signal(barrier, inc=1, device_id=(here.seq, here.same_core(k)), device_id_type=MESH)
    pl.semaphore_signal(barrier, inc=1, device_id=(here.seq, here.partner), device_id_type=MESH)

    order = reorder(own_rows).astype(bf16)
    values = tok_ref[...].astype(f32)
    normed = values * lax.rsqrt(jnp.mean(values * values, axis=-1, keepdims=True) + norm_epsilon) * gain_ref[...].reshape(1, width)
    shape = (SLABS, lanes, width)
    ng[here.chan // per_row, :, here.chan % per_row] = (
        dot_nn(order, normed.astype(bf16)).astype(bf16).reshape(shape)
    )
    pl.semaphore_wait(barrier, chips)
    first = Gather(
        here, ng, chips == 4, ag_send.at[0], ag_recv.at[0], ag_rsend.at[0], ag_rrecv.at[0], ag_fsend, ag_frecv
    )
    second = Gather(here, cg, False, ag_send.at[1], ag_recv.at[1], ag_rsend.at[1], ag_rrecv.at[1], None, None)
    first.start()

    cg[here.chan // per_row, :, here.chan % per_row] = dot_nn(order, cot_ref[...]).astype(bf16).reshape(shape)
    wxg[0:channels, :] = inw_ref[0].astype(bf16)
    wxg[channels:, :] = inw_ref[1].astype(bf16)
    row_masks(resets_ref, mask)
    rowf[...] = jnp.zeros_like(rowf)
    rowf[0 : KC + 3, :] = ch_ref[0 : KC + 3, :]
    rowf[DECAY_COL : DECAY_COL + DS, :] = -jnp.exp(ch_ref[KC + 3 :, :]) * LOG2E
    rowf[DT_COL : DT_COL + DR, :] = dtw_ref[...]
    table[...] = rowf[...].T
    for n in range(DS):
        decb[n] = jnp.broadcast_to(table[:, DECAY_COL + n : DECAY_COL + n + 1], (channels, LANES))
    padded[...] = jnp.zeros_like(padded)
    save(mask, mask_out)
    save(table, ct_out)
    save(decb, dec_out)

    step = SLABS // PIECES
    span = step * per_row * lanes

    def project(q):
        first.arrive(q)
        for r in range(rows_n):
            block = ng[r, q * step : (q + 1) * step].reshape(span, width)
            cols = slice((r * PIECES + q) * span, (r * PIECES + q + 1) * span)
            both = dot_nt(wxg[...], block)
            xs[:, cols] = both[0:channels]
            gs[:, cols] = both[channels:]

    if first.hop:
        for i in range(PIECES + 1):
            first.pass_on(i)
        for q in range(PIECES):
            project(q)
    else:
        first.pass_on(0)
        for q in range(PIECES):
            if q + 1 < PIECES:
                first.pass_on(q + 1)
            project(q)
    save(xs, x_out)
    save(ng, ng_out)

    high = tall(channels)

    def conv_tile(index, carry):
        i = index // rows_n
        r = index % rows_n
        rows = pl.ds(pl.multiple_of(i * high, high), high)
        taps = [jnp.broadcast_to(table[rows, k : k + 1], (high, LANES)) for k in range(KC + 1)]
        earlier = {s: pltpu.roll(xs[rows, t.cols(r, s)], 1, 1) for s in range(SLABS - KC + 1, SLABS)}
        for s in range(SLABS):
            conv = taps[KC]
            for j in range(KC):
                value = xs[rows, t.cols(r, s - j)] if s >= j else earlier[SLABS + s - j]
                if j > 0:
                    value = value * mask[j : j + 1, t.cols(r, s)]
                conv = conv + taps[KC - 1 - j] * value
            acts[rows, t.cols(r, s)] = (conv * jax.nn.sigmoid(conv)).astype(bf16)
        return carry

    lax.fori_loop(0, channels // high * rows_n, conv_tile, 0)
    part[...] = dot_nn(xw_ref[...].astype(bf16), acts[...])
    reduce = Reduce(here, part, from_pair, pair, from_chips, pj, rd_send, rd_recv)
    reduce.step1()
    save(acts, act_out)
    reduce.step2()

    def gate_tile(index, carry):
        i = index // rows_n
        r = index % rows_n
        rows = pl.ds(pl.multiple_of(i * 16, 16), 16)
        for s in range(SLABS):
            gate = gs[rows, t.cols(r, s)]
            sig = jax.nn.sigmoid(gate)
            gs[rows, t.cols(r, s)] = gate * sig
            slope[rows, t.cols(r, s)] = sig * (1.0 + gate * (1.0 - sig))
        return carry

    lax.fori_loop(0, channels // 16 * rows_n, gate_tile, 0)
    reduce.step3()
    reduce.step4()
    reduce.step5()
    second.start()
    save(pj, pj_out)

    padded[DT_COL : DT_COL + DR, :] = pj[0:DR, :]
    step_ref[...] = dot_nn(table[...].astype(bf16), padded[...])

    def prelude(index, carry):
        i = index // rows_n
        r = index % rows_n
        rows = pl.ds(pl.multiple_of(i * 16, 16), 16)
        bias = jnp.broadcast_to(table[rows, KC + 1 : KC + 2], (16, LANES))
        total = jnp.zeros((16, LANES), f32)
        for s in range(SLABS):
            cols = t.cols(r, s)
            value = softplus(step_ref[rows, cols] + bias)
            step_ref[rows, cols] = value
            du_ref[rows, cols] = value * acts[rows, cols].astype(f32)
            y_ref[rows, cols] = jnp.zeros((16, LANES), f32)
            total = total + jnp.where(mask[0:1, cols] > 0.0, HUGE, value)
        sums[pl.ds(pl.multiple_of(r * channels + i * 16, 16), 16), :] = total
        return carry

    lax.fori_loop(0, channels // 16 * rows_n, prelude, 0)
    windows(sums, wf, False)
    save(step_ref, step_out)
    expand = expand_matrix()

    def group(index, carry):
        r, j, i, g = t.split(index)
        rows = t.rows(i)
        nrows = pl.ds(pl.multiple_of(g * (NG * 8), NG * 8), NG * 8)

        @pl.when(j == 0)
        def _():
            if rows_n == 1:
                block = pj[DR:, :]
            else:
                block = pj[DR:, pl.ds(pl.multiple_of(r * SEQ_LEN, SEQ_LEN), SEQ_LEN)]
            b8[...] = dot_nn(expand, block[0:DS].astype(f32), highest)
            c8[...] = dot_nn(expand, block[DS:].astype(f32), highest)

        def tile(ref, s):
            return ref[rows, t.cols(r, s)].reshape(1, CT, 8, LANES)

        def state(ref, s):
            return ref[nrows, slab(s)].reshape(NG, 1, 8, LANES)

        dec = decb[pl.ds(g * NG, NG), rows, :].reshape(NG, CT, 8, LANES)
        h = jnp.zeros((NG, CT, 8, LANES), f32)
        for s in range(SLABS):
            stepk = jnp.where(mask[0:1, t.cols(r, s)] > 0.0, HUGE, step_ref[rows, t.cols(r, s)])
            a = jnp.exp2(dec * stepk.reshape(1, CT, 8, LANES))
            a_scr[s] = a
            h = a * h + state(b8, s) * tile(du_ref, s)
        at = pl.ds(pl.multiple_of(r * channels + i * t.span, t.span), t.span)
        for k in range(7):
            gain = jnp.exp2(dec * wf[k, at, :].reshape(1, CT, 8, LANES))
            h = h + gain * pltpu.roll(h, 1 << k, 3)
        h = pltpu.roll(h, 1, 3)
        h0[pl.ds(r * DS + g * NG, NG), rows, :] = h.reshape(NG, t.span, LANES)
        for s in range(SLABS):
            h = a_scr[s] * h + state(b8, s) * tile(du_ref, s)
            y_ref[rows, t.cols(r, s)] += jnp.sum(state(c8, s) * h, axis=0).reshape(t.span, LANES)
        return carry

    for segment in range(SEGMENTS):
        t.loop(segment, group)
        if segment + 2 >= SEGMENTS:
            for q in range(PIECES // 2):
                second.pass_on(q + (segment + 2 - SEGMENTS) * PIECES // 2)
    save(h0, h0_out)

    def skip_tile(index, carry):
        i = index // rows_n
        r = index % rows_n
        rows = pl.ds(pl.multiple_of(i * 16, 16), 16)
        skip = jnp.broadcast_to(table[rows, KC + 2 : KC + 3], (16, LANES))
        for s in range(SLABS):
            cols = t.cols(r, s)
            y = y_ref[rows, cols] + skip * acts[rows, cols].astype(f32)
            gated[rows, cols] = (y * gs[rows, cols]).astype(bf16)
            y_ref[rows, cols] = y * slope[rows, cols]
        return carry

    lax.fori_loop(0, channels // 16 * rows_n, skip_tile, 0)
    save(gated, gated_out)
    low = outw_ref[...].astype(bf16)
    for q in range(PIECES):
        second.arrive(q)
        for r in range(rows_n):
            block = cg[r, q * step : (q + 1) * step].reshape(span, width)
            cols = slice((r * PIECES + q) * span, (r * PIECES + q + 1) * span)
            dgs[:, cols] = dot_nt(low, block)
    save(cg, cg_out)

    def grad_tile(index, carry):
        i = index // rows_n
        r = index % rows_n
        rows = pl.ds(pl.multiple_of(i * 16, 16), 16)
        for s in range(SLABS):
            cols = t.cols(r, s)
            dg = dgs[rows, cols]
            dgate[rows, cols] = (dg * y_ref[rows, cols]).astype(bf16)
            dgs[rows, cols] = dg * gs[rows, cols]
        return carry

    lax.fori_loop(0, channels // 16 * rows_n, grad_tile, 0)
    save(dgs, dy_out)
    save(dgate, dgate_out)
    first.close()
    second.close()
    reduce.close()
    for c in copies:
        c.wait()


def front_call(chan_size, tokens, cotangent, gain, in_weight, x_weight, out_weight, chan_params, dt_weight, resets):
    own_rows, width = tokens.shape
    count = resets.shape[0] * LANES
    channels = out_weight.shape[0]
    chips = chan_size // 2
    rows = count // SEQ_LEN
    wide = (channels, count)
    whole = (rows, SLABS, SEQ_LEN // own_rows, own_rows // SLABS, width)
    project = DR + 2 * DS
    any_spec = pl.BlockSpec(memory_space=pl.ANY)
    vmem = pl.BlockSpec(memory_space=pltpu.VMEM)
    dma = pltpu.SemaphoreType.DMA
    gather_sems = (2, chips, PIECES)
    states = (rows * DS, channels, LANES)
    decays = (DS, channels, LANES)
    outs = [
        (wide, f32), (wide, bf16), (wide, f32), (wide, f32), (wide, bf16), (wide, bf16), ((project, count), bf16),
        (whole, bf16), (whole, bf16), (states, f32), (decays, f32), ((4, count), f32), ((channels, LANES), f32),
    ]
    scratch = [
        (whole, bf16), (whole, bf16), (wide, f32), (wide, f32), (wide, f32), (wide, bf16), (wide, f32),
        ((2 * channels, width), bf16),
        ((project, count), f32), ((project, count // 2), f32), ((project, count // 2), bf16),
        ((chips - 1, project, count // 2 // chips), bf16), ((project, count), bf16),
        ((4, count), f32), ((channels, LANES), f32), ((LANES, channels), f32), ((LANES, count), bf16),
        (wide, f32), (wide, f32), (wide, f32), ((rows * channels, LANES), f32), ((7, rows * channels, LANES), f32),
        ((DS * 8, SEQ_LEN), f32), ((DS * 8, SEQ_LEN), f32), (decays, f32), (states, f32),
        ((SLABS, NG, CT, 8, LANES), f32), (wide, bf16), (wide, bf16),
    ]
    return pl.pallas_call(
        functools.partial(front_kernel, chan_size),
        in_specs=[vmem] * 9,
        out_specs=[any_spec] * len(outs),
        out_shape=[jax.ShapeDtypeStruct(*o) for o in outs],
        scratch_shapes=[pltpu.VMEM(*s) for s in scratch]
        + [dma(gather_sems)] * 4
        + [dma((PIECES,))] * 2
        + [dma((2 * chips,))] * 2
        + [dma((len(outs),))],
        compiler_params=pltpu.CompilerParams(collective_id=0, has_side_effects=True, vmem_limit_bytes=60 * MIB),
        name="front",
    )(tokens, cotangent, gain, in_weight, x_weight, out_weight, chan_params, dt_weight, resets)


def back_kernel(
    chan_size, seq_size,
    table, mask, xw_ref,
    gated_in, outw_in, cot_in, step_in, act_in, pj_in, dec_in, dy_in, h0_in, dgate_in, normed_in, inw_in, x_in,
    msum_ref, dsum_ref, za_out, zb_out, zc_out, gsum_ref,
    gated, outw, step_ref, act, pjf, decb, dy, h0, dgate, inw, rows_buf, low, dx, dc, taps_red, gin1,
    du, s1, ds2, totals, wb, b8, c8, db8, dc8, red, a_scr, ah_scr, pback,
    part, pair_buf, land, from_pair, pair, from_chips, pj,
    za, zb, zc, zha, zhb, zhc, gp, gz, gc,
    in_sem, out_sem, m_s1, m_r1, m_s2, m_r2, d_s1, d_r1, d_s2, d_r2,
    rd_send, rd_recv, z_send, z_recv, gz_send, gz_recv, gc_send, gc_recv,
):
    here = Here(chan_size)
    channels, tokens = gated.shape
    rows_n = pair_buf.shape[0]
    width = outw.shape[1]
    project = pj.shape[0]
    t = Tiles(channels, rows_n)
    tile_count = channels // 16 * rows_n

    loads = {}
    for index, (name, src, dst) in enumerate(
        (
            ("gated", gated_in, gated), ("outw", outw_in, outw), ("cot", cot_in.at[0], rows_buf.at[0]),
            ("step", step_in, step_ref), ("act", act_in, act), ("pj", pj_in, pjf), ("dec", dec_in, decb),
            ("dy", dy_in, dy), ("h0", h0_in, h0), ("dgate", dgate_in, dgate),
            ("normed", normed_in.at[0], rows_buf.at[1]), ("inw", inw_in, inw), ("x", x_in, du),
        )
    ):
        loads[name] = pltpu.make_async_copy(src, dst, in_sem.at[index])
    early = ("gated", "outw", "cot")
    for name in early:
        loads[name].start()

    barrier = pltpu.get_barrier_semaphore()
    for k in range(1, chan_size):
        pl.semaphore_signal(barrier, inc=1, device_id=(here.seq, flip(here.chan, k)), device_id_type=MESH)
    for k in range(1, seq_size):
        pl.semaphore_signal(barrier, inc=1, device_id=(flip(here.seq, k), here.chan), device_id_type=MESH)

    reduce = Reduce(here, pback, from_pair, pair, from_chips, pj, rd_send, rd_recv)
    mixed = Scatter(here, part, pair_buf, land, m_s1, m_r1, m_s2, m_r2)
    normed_grad = Scatter(here, part, pair_buf, land, d_s1, d_r1, d_s2, d_r2)
    sum_a = SeqSum(here, seq_size, za, zha, z_send.at[0], z_recv.at[0])
    sum_b = SeqSum(here, seq_size, zb, zhb, z_send.at[1], z_recv.at[1])
    sum_c = SeqSum(here, seq_size, zc, zhc, z_send.at[2], z_recv.at[2])
    if za.shape[0] > channels:
        for buf in (za, zb, zc):
            buf[channels:, :] = jnp.zeros((buf.shape[0] - channels, buf.shape[1]), bf16)

    def row_block(slot):
        return rows_buf[slot].reshape(SEQ_LEN, width)

    def row_cols(r):
        return slice(r * SEQ_LEN, (r + 1) * SEQ_LEN)

    def fetch(src, r, slot, name):
        index = list(loads).index(name)
        c = pltpu.make_async_copy(src.at[r], rows_buf.at[slot], in_sem.at[index])
        c.start()
        return c

    loads["gated"].wait()
    loads["outw"].wait()
    for name in loads:
        if name not in early and name != "x":
            loads[name].start()
    low[0] = outw[...].astype(bf16)
    pl.semaphore_wait(barrier, chan_size - 1 + seq_size - 1)
    mixed.produce(lambda cols: dot_tn(gated[:, cols], low[0]), False, None)
    loads["cot"].wait()
    out_grad = dot_nn(gated[:, row_cols(0)], row_block(0))
    for r in range(1, rows_n):
        fetch(cot_in, r, 0, "cot").wait()
        out_grad = out_grad + dot_nn(gated[:, row_cols(r)], row_block(0))
    za[0:channels, :] = out_grad.astype(bf16)
    sum_a.start()
    loads["dgate"].wait()
    loads["normed"].wait()
    in_grad = dot_nn(dgate[:, row_cols(0)], row_block(1))
    for r in range(1, rows_n):
        fetch(normed_in, r, 1, "normed").wait()
        in_grad = in_grad + dot_nn(dgate[:, row_cols(r)], row_block(1))
    gin1[...] = in_grad
    zb[0:channels, :] = in_grad.astype(bf16)
    sum_b.start()
    loads["inw"].wait()
    low[0] = inw[0].astype(bf16)
    low[1] = inw[1].astype(bf16)

    for name in ("step", "act", "pj", "dec", "dy", "h0"):
        loads[name].wait()
    red[...] = jnp.zeros_like(red)

    def prelude(index, carry):
        i = index // rows_n
        r = index % rows_n
        rows = pl.ds(pl.multiple_of(i * 16, 16), 16)
        total = jnp.zeros((16, LANES), f32)
        for s in range(SLABS):
            cols = t.cols(r, s)
            value = step_ref[rows, cols]
            du[rows, cols] = value * act[rows, cols].astype(f32)
            s1[rows, cols] = jnp.zeros((16, LANES), f32)
            ds2[rows, cols] = jnp.zeros((16, LANES), f32)
            total = total + jnp.where(mask[0:1, cols] > 0.0, HUGE, value)
        totals[pl.ds(pl.multiple_of(r * channels + i * 16, 16), 16), :] = total
        return carry

    lax.fori_loop(0, tile_count, prelude, 0)
    windows(totals, wb, True)
    for q in range(PIECES):
        mixed.send(q)
    expand = expand_matrix()

    def group(index, carry):
        r, j, i, g = t.split(index)
        rows = t.rows(i)
        nrows = pl.ds(pl.multiple_of(g * (NG * 8), NG * 8), NG * 8)
        whole_row = slice(0, SEQ_LEN) if rows_n == 1 else pl.ds(pl.multiple_of(r * SEQ_LEN, SEQ_LEN), SEQ_LEN)

        @pl.when(j == 0)
        def _():
            block = pjf[DR:, whole_row]
            b8[...] = dot_nn(expand, block[0:DS].astype(f32), highest)
            c8[...] = dot_nn(expand, block[DS:].astype(f32), highest)
            db8[...] = jnp.zeros_like(db8)
            dc8[...] = jnp.zeros_like(dc8)

        def tile(ref, s):
            return ref[rows, t.cols(r, s)].reshape(1, CT, 8, LANES)

        def state(ref, s):
            return ref[nrows, slab(s)].reshape(NG, 1, 8, LANES)

        dec = decb[pl.ds(g * NG, NG), rows, :].reshape(NG, CT, 8, LANES)
        h = h0[pl.ds(r * DS + g * NG, NG), rows, :].reshape(NG, CT, 8, LANES)
        for s in range(SLABS):
            stepk = jnp.where(mask[0:1, t.cols(r, s)] > 0.0, HUGE, step_ref[rows, t.cols(r, s)])
            a = jnp.exp2(dec * stepk.reshape(1, CT, 8, LANES))
            a_scr[s] = a
            ah = a * h
            ah_scr[s] = ah
            h = ah + state(b8, s) * tile(du, s)
            dc8[nrows, slab(s)] += jnp.sum(tile(dy, s) * h, axis=1).reshape(NG * 8, LANES)
        p = jnp.zeros((NG, CT, 8, LANES), f32)
        for s in reversed(range(SLABS)):
            p = a_scr[s] * (tile(dy, s) * state(c8, s) + p)
        at = pl.ds(pl.multiple_of(r * channels + i * t.span, t.span), t.span)
        for k in range(7):
            gain = jnp.exp2(dec * wb[k, at, :].reshape(1, CT, 8, LANES))
            p = p + gain * pltpu.roll(p, LANES - (1 << k), 3)
        p = pltpu.roll(p, LANES - 1, 3)
        rate = jnp.zeros((NG, CT, 8, LANES), f32)
        for s in reversed(range(SLABS)):
            lam = tile(dy, s) * state(c8, s) + p
            p = a_scr[s] * lam
            s1[rows, t.cols(r, s)] += jnp.sum(lam * state(b8, s), axis=0).reshape(t.span, LANES)
            db8[nrows, slab(s)] += jnp.sum(lam * tile(du, s), axis=1).reshape(NG * 8, LANES)
            q = lam * ah_scr[s]
            ds2[rows, t.cols(r, s)] += jnp.sum(dec * q, axis=0).reshape(t.span, LANES)
            rate = rate + q * tile(step_ref, s)
        for n in range(NG):
            cols = pl.ds(pl.multiple_of((g * NG + n) * LANES, LANES), LANES)
            red[rows, cols] += rate[n].reshape(t.span, LANES)

        @pl.when(j == t.per_row - 1)
        def _():
            pback[DR : DR + DS, whole_row] = dot_tn(expand, db8[...], highest).astype(bf16)
            pback[DR + DS :, whole_row] = dot_tn(expand, dc8[...], highest).astype(bf16)

        return carry

    levels = seq_size.bit_length() - 1
    for segment in range(SEGMENTS):
        t.loop(segment, group)
        if segment == 1:
            sum_a.step(0)
            sum_b.step(0)
        if segment + 1 == SEGMENTS:
            for i in range(1, levels):
                sum_a.step(i)
                sum_b.step(i)
            mixed.finish(msum_ref)
    loads["x"].start()
    x_buf = du

    def adjoint_tile(index, carry):
        i = index // rows_n
        r = index % rows_n
        rows = pl.ds(pl.multiple_of(i * 16, 16), 16)
        skip = jnp.broadcast_to(table[rows, KC + 2 : KC + 3], (16, LANES))
        skip_sum = jnp.zeros((16, LANES), f32)
        bias_sum = jnp.zeros((16, LANES), f32)
        for s in range(SLABS):
            cols = t.cols(r, s)
            value = step_ref[rows, cols]
            lam_b = s1[rows, cols]
            d_y = dy[rows, cols]
            act_s = act[rows, cols].astype(f32)
            s1[rows, cols] = d_y * skip + lam_b * value
            small = value * (1.0 - value * (0.5 - value * (1.0 / 6.0)))
            slope = jnp.where(value < 0.01, small, 1.0 - jnp.exp(-value))
            back = ((lam_b * act_s + LN2 * ds2[rows, cols]) * slope).astype(bf16)
            dx[rows, cols] = back
            skip_sum = skip_sum + d_y * act_s
            bias_sum = bias_sum + back.astype(f32)
        red[rows, DS * LANES : (DS + 1) * LANES] += skip_sum
        red[rows, (DS + 1) * LANES :] += bias_sum
        return carry

    lax.fori_loop(0, tile_count, adjoint_tile, 0)
    low_table = table[...].astype(bf16)
    for r in range(rows_n):
        pback[0:DR, row_cols(r)] = dot_tn(low_table, dx[:, row_cols(r)])[DT_COL : DT_COL + DR].astype(bf16)
    reduce.step1()
    pick = jnp.where(iota(((DS + 2) * LANES, LANES), 0) // LANES == iota(((DS + 2) * LANES, LANES), 1), 1.0, 0.0)
    dt_grad = jnp.concatenate(
        [
            jnp.zeros((channels, DT_COL), f32),
            dot_nt(dx[...], pjf[0:DR, :]),
            jnp.zeros((channels, LANES - DT_COL - DR), f32),
        ],
        axis=1,
    )
    zc[0:channels, width + LANES :] = (dot_nn(red[...], pick, highest) + dt_grad).astype(bf16)
    reduce.step2()
    reduce.step3()
    reduce.step4()
    saves = sum_a.finish(za_out, out_sem.at[0])
    saves += sum_b.finish(zb_out, out_sem.at[1])
    loads["x"].wait()
    x_low = xw_ref[...].astype(bf16)
    reduce.step5()
    for r in range(rows_n):
        s1[:, row_cols(r)] += dot_tn(x_low, pj[:, row_cols(r)])

    high = tall(channels)

    def conv_tile(index, carry):
        i = index // rows_n
        r = index % rows_n
        rows = pl.ds(pl.multiple_of(i * high, high), high)
        taps = [jnp.broadcast_to(table[rows, k : k + 1], (high, LANES)) for k in range(KC + 1)]
        earlier = {s: pltpu.roll(x_buf[rows, t.cols(r, s)], 1, 1) for s in range(SLABS - KC + 1, SLABS)}
        sums = [jnp.zeros((high, LANES), f32) for _ in range(KC + 1)]
        for s in range(SLABS):
            cols = t.cols(r, s)
            inputs = []
            conv = taps[KC]
            for j in range(KC):
                value = x_buf[rows, t.cols(r, s - j)] if s >= j else earlier[SLABS + s - j]
                if j > 0:
                    value = value * mask[j : j + 1, cols]
                inputs.append(value)
                conv = conv + taps[KC - 1 - j] * value
            sig = jax.nn.sigmoid(conv)
            d_conv = s1[rows, cols] * (sig * (1.0 + conv * (1.0 - sig)))
            dc[:, slab(s)] = d_conv
            for j in range(KC):
                sums[KC - 1 - j] = sums[KC - 1 - j] + d_conv * inputs[j]
            sums[KC] = sums[KC] + d_conv
        wrapped = {}
        for s in range(KC - 1):
            for j in range(s + 1, KC):
                wrapped[s, j] = pltpu.roll(dc[:, slab(s)] * mask[j : j + 1, t.cols(r, s)], LANES - 1, 1)
        for s in range(SLABS):
            d_x = taps[KC - 1] * dc[:, slab(s)]
            for j in range(1, KC):
                if s + j < SLABS:
                    value = dc[:, slab(s + j)] * mask[j : j + 1, t.cols(r, s + j)]
                else:
                    value = wrapped[s + j - SLABS, j]
                d_x = d_x + taps[KC - 1 - j] * value
            dx[rows, t.cols(r, s)] = d_x.astype(bf16)
        for k in range(KC + 1):
            @pl.when(r == 0)
            def _():
                taps_red[rows, slab(k)] = sums[k]

            @pl.when(r > 0)
            def _():
                taps_red[rows, slab(k)] += sums[k]
        return carry

    lax.fori_loop(0, channels // high * rows_n, conv_tile, 0)

    def weight_sums():
        if rows_n > 1:
            fetch(normed_in, 0, 1, "normed").wait()
        in_grad = dot_nn(dx[:, row_cols(0)], row_block(1))
        for r in range(1, rows_n):
            fetch(normed_in, r, 1, "normed").wait()
            in_grad = in_grad + dot_nn(dx[:, row_cols(r)], row_block(1))
        zc[0:channels, 0:width] = in_grad.astype(bf16)
        x_grad = dot_nt(act[...], pj[...])
        x_grad = jnp.concatenate([x_grad, jnp.zeros((channels, LANES - project), f32)], axis=1)
        k_i = iota(((KC + 1) * LANES, LANES), 0)
        pick = jnp.where(k_i // LANES + project == iota(((KC + 1) * LANES, LANES), 1), 1.0, 0.0)
        zc[0:channels, width : width + LANES] = (x_grad + dot_nn(taps_red[...], pick, highest)).astype(bf16)
        sum_c.start()

        both = low[0].astype(f32) * in_grad + low[1].astype(f32) * gin1[...]
        gp[...] = jnp.sum(both.reshape(channels // 8, 8, width), axis=0)

    normed_grad.produce(
        lambda cols: dot_tn(dx[:, cols], low[0]) + dot_tn(dgate[:, cols], low[1]), True, weight_sums
    )
    normed_grad.send(PIECES - 1)

    def gain_seq(k):
        return pltpu.make_async_remote_copy(
            src_ref=gp, dst_ref=gz.at[k - 1], send_sem=gz_send.at[k - 1], recv_sem=gz_recv.at[k - 1],
            device_id=(flip(here.seq, k), here.chan), device_id_type=MESH,
        )

    def gain_chan(k):
        return here.copy(gz.at[seq_size - 1], gc.at[k - 1], gc_send.at[k - 1], gc_recv.at[k - 1], flip(here.chan, k))

    for k in range(1, seq_size):
        gain_seq(k).start()
    for k in range(1, seq_size):
        gain_seq(k).wait()
    total = gp[...]
    for k in range(1, seq_size):
        total = total + gz[k - 1]
    gz[seq_size - 1] = total
    for k in range(1, chan_size):
        gain_chan(k).start()
    for i in range(levels):
        sum_c.step(i)
    for k in range(1, chan_size):
        gain_chan(k).wait()
        total = total + gc[k - 1]
    gsum_ref[...] = total
    normed_grad.finish(dsum_ref)
    saves += sum_c.finish(zc_out, out_sem.at[2])
    reduce.close()
    for c in saves:
        c.wait()


def back_call(
    chan_size, seq_size, own_rows, table, masks, x_weight, gated, out_weight, cot_all, step, act, pj, decays, dy, h0,
    dgate, normed_all, in_weight, x_cols,
):
    channels, width = out_weight.shape
    count = masks.shape[1]
    chips = chan_size // 2
    rows = count // SEQ_LEN
    per_row = SEQ_LEN // own_rows // 2
    lanes = own_rows // SLABS
    project = DR + 2 * DS
    wide = (channels, count)
    padded = (channels + 31) // 32 * 32
    levels = seq_size.bit_length() - 1
    any_spec = pl.BlockSpec(memory_space=pl.ANY)
    vmem = pl.BlockSpec(memory_space=pltpu.VMEM)
    dma = pltpu.SemaphoreType.DMA
    sums = ((padded, width), (padded, width), (padded, width + 2 * LANES))
    states = (DS * 8, SEQ_LEN)
    loops = (SLABS, NG, CT, 8, LANES)
    outs = [
        ((own_rows, width), f32), ((own_rows, width), f32), (sums[0], bf16), (sums[1], bf16), (sums[2], bf16),
        ((8, width), f32),
    ]
    scratch = [
        (wide, bf16), ((channels, width), f32), (wide, f32), (wide, bf16), ((project, count), bf16),
        ((DS, channels, LANES), f32), (wide, f32), ((rows * DS, channels, LANES), f32), (wide, bf16),
        ((2, channels, width), f32), ((2, SLABS, 2 * per_row, lanes, width), bf16),
        ((2, channels, width), bf16), (wide, bf16), ((tall(channels), SEQ_LEN), f32), ((channels, (KC + 1) * LANES), f32),
        ((channels, width), f32),
        (wide, f32), (wide, f32), (wide, f32), ((rows * channels, LANES), f32), ((7, rows * channels, LANES), f32),
        (states, f32), (states, f32), (states, f32), (states, f32), ((channels, (DS + 2) * LANES), f32),
        (loops, f32), (loops, f32), ((project, count), bf16),
        ((min(rows, 2), SLABS, per_row, 2, lanes, width), bf16), ((rows, SLABS, per_row, lanes, width), bf16),
        ((chips - 1, SLABS, lanes, width), bf16), ((project, count // 2), bf16), ((project, count // 2), bf16),
        ((chips - 1, project, count // 2 // chips), bf16), ((project, count), bf16),
        (sums[0], bf16), (sums[1], bf16), (sums[2], bf16),
    ]
    scratch += [((levels + 1, padded // 2, s[1]), bf16) for s in sums]
    scratch += [((8, width), f32), ((seq_size, 8, width), f32), ((chan_size - 1, 8, width), f32)]
    return pl.pallas_call(
        functools.partial(back_kernel, chan_size, seq_size),
        in_specs=[vmem] * 3 + [any_spec] * 13,
        out_specs=[vmem, vmem, any_spec, any_spec, any_spec, vmem],
        out_shape=[jax.ShapeDtypeStruct(*o) for o in outs],
        scratch_shapes=[pltpu.VMEM(*s) for s in scratch]
        + [dma((13,)), dma((3, 2))]
        + ([dma((rows * PIECES,))] * 2 + [dma((chips * PIECES,))] * 2) * 2
        + [dma((2 * chips,))] * 2
        + [dma((3, levels + 1))] * 2
        + [dma((seq_size,))] * 2
        + [dma((chan_size,))] * 2,
        compiler_params=pltpu.CompilerParams(collective_id=1, has_side_effects=True, vmem_limit_bytes=60 * MIB),
        name="back",
    )(
        table, masks, x_weight, gated, out_weight, cot_all, step, act, pj, decays, dy, h0, dgate, normed_all, in_weight, x_cols
    )


def update(grad, master, first, second, rate, outs):
    new = adamw_core(master, first, second, grad, rate)
    for ref, value in zip(outs, new):
        ref[...] = value
    outs[3][...] = new[0].astype(bf16)


def finish_kernel(
    tok_ref, cot_ref, msum_ref, dsum_ref, za_ref, zb_ref, zc_ref, zb_all, zc_all, gsum_ref,
    gain_m, gain_f, gain_s, in_m, in_f, in_s, x_m, x_f, x_s, dt_m, dt_f, dt_s, out_m, out_f, out_s, ch_m, ch_f, ch_s,
    mixed_ref, tgrad_ref, *rest,
):
    gain_o, in_o, x_o, dt_o, out_o, ch_o = (rest[i * 4 : i * 4 + 4] for i in range(6))
    ch_grad = rest[24]
    i = pl.program_id(0)
    width = tok_ref.shape[1]
    own_rows = msum_ref.shape[0]
    block = tok_ref.shape[0]
    lanes = own_rows // SLABS
    channels = x_m.shape[1]

    r = lax.broadcasted_iota(jnp.int32, (block, own_rows), 0) + i * block
    q = lax.broadcasted_iota(jnp.int32, (block, own_rows), 1)
    order = jnp.where(r == (q % lanes) * SLABS + q // lanes, 1.0, 0.0).astype(bf16)

    def in_order(ref):
        values = ref[...]
        high = values.astype(bf16)
        return dot_nn(order, high) + dot_nn(order, (values - high.astype(f32)).astype(bf16))

    values = tok_ref[...].astype(f32)
    mixed_ref[...] = (values + in_order(msum_ref)).astype(bf16)
    d_normed = in_order(dsum_ref)
    rstd = lax.rsqrt(jnp.mean(values * values, axis=-1, keepdims=True) + norm_epsilon)
    gain_row = gain_m[...].reshape(1, width)
    scaled = gain_row * d_normed
    mean = jnp.mean(scaled * values, axis=-1, keepdims=True)
    tgrad_ref[...] = cot_ref[...].astype(f32) + rstd * scaled - values * (rstd * rstd * rstd * mean)

    out_grad = za_ref[...].astype(f32)
    update(out_grad, out_m[...], out_f[...], out_s[...], rate_output, out_o)
    for k, ref in ((0, zc_ref), (1, zb_ref)):
        grad = ref[:, 0:width].astype(f32)
        new = adamw_core(in_m[k], in_f[k], in_s[k], grad, rate_inner)
        for o, value in zip(in_o, new):
            o[k] = value
        in_o[3][k] = new[0].astype(bf16)

    @pl.when(i == 0)
    def _():
        grad_b = zb_all[...].astype(f32).T
        grad_c = zc_all[...].astype(f32).T
        update(grad_b[64 : 64 + DR, 0:channels], dt_m[...], dt_f[...], dt_s[...], rate_step, dt_o)
        project = x_m.shape[0]
        update(grad_c[0:project, 0:channels], x_m[...], x_f[...], x_s[...], rate_project, x_o)
        ch_grad[0 : KC + 1, :] = grad_c[project : project + KC + 1, 0:channels]
        ch_grad[KC + 1 : KC + 2, :] = grad_b[DS + 1 : DS + 2, 0:channels]
        ch_grad[KC + 2 : KC + 3, :] = grad_b[DS : DS + 1, 0:channels]
        ch_grad[KC + 3 :, :] = grad_b[0:DS, 0:channels] * -jnp.exp(ch_m[KC + 3 :, :])
        update(ch_grad[...], ch_m[...], ch_f[...], ch_s[...], rate_channel, ch_o)
        gain_grad = jnp.sum(gsum_ref[...], axis=0, keepdims=True) / gain_row
        moments = (ref[...].reshape(1, width) for ref in (gain_f, gain_s))
        new = adamw_core(gain_row, *moments, gain_grad, rate_gain)
        for ref, value in zip(gain_o, (*new, new[0].astype(bf16))):
            ref[...] = value.reshape(width)


def finish_call(tokens, cotangent, msum, dsum, za, zb, zc, gsum, gains, inners, projects, steps, outputs, chans):
    own_rows, width = tokens.shape
    channels = outputs[0].shape[0]
    cb = 96 if channels % 96 == 0 else channels
    grid = channels // cb
    block = own_rows // grid
    row = pl.BlockSpec((block, width), lambda i: (i, 0))

    def full(shape):
        return pl.BlockSpec(shape, lambda i: (0,) * len(shape))

    inner = pl.BlockSpec((2, cb, width), lambda i: (0, i, 0))
    outer = pl.BlockSpec((cb, width), lambda i: (i, 0))
    tails = [pl.BlockSpec((zc.shape[0], LANES), lambda i, k=k: (0, width // LANES + k)) for k in (1, 0)]
    zed = pl.BlockSpec((cb, width), lambda i: (i, 0))
    groups = (gains, inners, projects, steps, outputs, chans)
    specs = (full(gains[0].shape), inner, full(projects[0].shape), full(steps[0].shape), outer, full(chans[0].shape))
    in_specs = [row, row, full(msum.shape), full(dsum.shape), zed, zed, zed, *tails, full(gsum.shape)]
    out_specs = [row, row]
    out_shape = [jax.ShapeDtypeStruct(tokens.shape, bf16), jax.ShapeDtypeStruct(tokens.shape, f32)]
    args = [tokens, cotangent, msum, dsum, za, zb, zc, zc, zc, gsum]
    for arrays, spec in zip(groups, specs):
        in_specs += [spec] * 3
        out_specs += [spec] * 4
        out_shape += [jax.ShapeDtypeStruct(arrays[0].shape, f32)] * 3 + [jax.ShapeDtypeStruct(arrays[0].shape, bf16)]
        args += list(arrays)
    return pl.pallas_call(
        finish_kernel,
        grid=(grid,),
        in_specs=in_specs,
        out_specs=out_specs,
        out_shape=out_shape,
        scratch_shapes=[pltpu.VMEM(chans[0].shape, f32)],
        compiler_params=pltpu.CompilerParams(dimension_semantics=("arbitrary",), vmem_limit_bytes=60 * MIB),
        name="finish",
    )(*args)


def per_device(
    tokens,
    resets,
    cotangent,
    norm_gain,
    in_weight,
    x_weight,
    dt_weight,
    out_weight,
    chan_params,
    gain_first,
    gain_second,
    in_first,
    in_second,
    x_first,
    x_second,
    dt_first,
    dt_second,
    out_first,
    out_second,
    chan_first,
    chan_second,
):
    own_count = tokens.shape[0]
    chan_size = lax.axis_size("chan")
    seq_size = lax.axis_size("seq")
    inners = [jnp.swapaxes(a, 1, 2) for a in (in_weight, in_first, in_second)]
    projects = [a.T for a in (x_weight, x_first, x_second)]
    x_cols, act, step, dy, gated, dgate, pj, normed_all, cot_all, h0, decays, masks, table = front_call(
        chan_size, tokens, cotangent, norm_gain, inners[0], projects[0], out_weight, chan_params, dt_weight,
        resets.reshape(-1, LANES),
    )
    msum, dsum, za, zb, zc, gsum = back_call(
        chan_size, seq_size, own_count, table, masks, projects[0], gated, out_weight, cot_all, step, act, pj, decays, dy, h0,
        dgate, normed_all, inners[0], x_cols,
    )
    result = finish_call(
        tokens, cotangent, msum, dsum, za, zb, zc, gsum,
        (norm_gain, gain_first, gain_second),
        inners,
        projects,
        (dt_weight, dt_first, dt_second),
        (out_weight, out_first, out_second),
        (chan_params, chan_first, chan_second),
    )
    result = list(result)
    result[6:10] = [jnp.swapaxes(a, 1, 2) for a in result[6:10]]
    result[10:14] = [a.T for a in result[10:14]]
    return tuple(result)


def solution(mesh):
    rows = P(("seq", "chan"), None)
    inner = P(None, None, "chan")
    by_row = P("chan", None)
    by_col = P(None, "chan")
    placed = (rows, P("seq"), rows, P(), inner, by_row, by_col, by_row, by_col, P(), P())
    placed += (inner, inner, by_row, by_row, by_col, by_col, by_row, by_row, by_col, by_col)
    return jax.shard_map(
        per_device,
        mesh=mesh,
        in_specs=placed,
        out_specs=(rows, rows)
        + (P(),) * 4
        + (inner,) * 4
        + (by_row,) * 4
        + (by_col,) * 4
        + (by_row,) * 4
        + (by_col,) * 4,
        check_vma=False,
    )
```

profile of v0, /device:TPU:0, one launch (start us, length us, event | category | flops | bytes accessed | tf_op | source)
XLA Modules:
  0.0 160.4 jit_solution(6263922970359990758)
XLA Ops:
  0.7 61.8 %front.1 = (f32[192,2048]{1,0:T(8,128)}, bf16[192,2048]{1,0:T(8,128)(2,1)}, f32[192,2048]{1,0:T(8,128)}, f32[192,2048]{1,0:T(8,128)}, bf16[192,2048]{1,0:T(8,128...) custom-call(bf16[256,768]{1,0:T(8,128)(2,1)} %tok_ref.3, ...), custom_call_target="tpu_custom_call" | custom-call | tf_op jit(solution)/shard_map/front/pallas_call | solution.py:737
  62.5 88.7 %back.1 = (f32[256,768]{1,0:T(8,128)}, f32[256,768]{1,0:T(8,128)}, bf16[192,768]{1,0:T(8,128)(2,1)}, bf16[192,768]{1,0:T(8,128)(2,1)}, bf16[192,1024]{1,0:T(8,128)(2,1)}, /*index=5*/f32[8,768]{1,0:T(8,128)}) custom-call(f32[192,128]{1,0:T(8,128)} %get-tuple-element.71.table, f32[4,2048]{1,0:T(4,128)} %get-tuple-element.72.mask, f32[80,192]{1,0:T(8,128)} %bitcast.21, ...), custom_call_target="tpu_custom_call" | custom-call | tf_op jit(solution)/shard_map/back/pallas_call | solution.py:1134
  151.2 8.9 %finish.1 = (bf16[256,768]{1,0:T(8,128)(2,1)}, f32[256,768]{1,0:T(8,128)}, f32[768]{0:T(1024)}, f32[768]{0:T(1024)}, f32[768]{0:T(1024)}, /*index=5*/bf16[768]{0...) custom-call(bf16[256,768]{1,0:T(8,128)(2,1)} %tok_ref.3, ...), custom_call_target="tpu_custom_call" | custom-call | tf_op jit(solution)/shard_map/finish/pallas_call | solution.py:1246
where the time goes:
time: 163 us; the launch traced here: 160 us
  Pallas kernels  159 us (98%)
    pallas_call x1, Pallas kernels, back_call(): pl.pallas_call(functools.partial(back_kernel, chan_size, seq_size), in_sp...  88.7 us
    pallas_call x1, Pallas kernels, front_call(): pl.pallas_call(functools.partial(front_kernel, chan_size), in_specs=[vmem...  61.8 us
    pallas_call x1, Pallas kernels, finish_call(): pl.pallas_call(finish_kernel, grid=(grid,), in_specs=in_specs, out_specs=...  8.91 us

commit v1 on v0

--- a/solution.py
+++ b/solution.py
@@ -14,10 +14,8 @@
 STEP = 10
 SLABS = 16
 LANES = 128
-NG = 16
-CT = 2
-SEGMENTS = 4
-PIECES = 4
+NG = 4
+PIECES = 2
 MIB = 1024 * 1024
 MESH = pl.DeviceIdType.MESH
 
@@ -442,16 +440,22 @@
     return jnp.where(iota((DS * 8, DS), 0) // 8 == iota((DS * 8, DS), 1), 1.0, 0.0)
 
 
+def lane_scan(values, decay, window_ref, at, later):
+    for k in range(7):
+        gain = jnp.exp2(decay * window_ref[k, at, :][None])
+        values = values + gain * pltpu.roll(values, LANES - (1 << k) if later else 1 << k, 2)
+    return pltpu.roll(values, LANES - 1 if later else 1, 2)
+
+
+def tile_depth(rows_n):
+    return 2 if rows_n == 1 else 1
+
+
 class Tiles:
     def __init__(self, channels, rows_n):
-        self.rows_n, self.span = rows_n, CT * 8
-        self.tiles, self.groups = channels // self.span, DS // NG
-        self.per_row = self.tiles * self.groups
-        self.count = rows_n * self.per_row
-
-    def split(self, index):
-        r, j = (0, index) if self.rows_n == 1 else (index // self.per_row, index % self.per_row)
-        return r, j, j // self.groups, j % self.groups
+        self.ct = tile_depth(rows_n)
+        self.rows_n, self.span = rows_n, self.ct * 8
+        self.tiles = channels // self.span
 
     def rows(self, i):
         return pl.ds(pl.multiple_of(i * self.span, self.span), self.span)
@@ -461,9 +465,16 @@
             return slab(s)
         return pl.ds(pl.multiple_of(r * SEQ_LEN + s * LANES, LANES), LANES)
 
-    def loop(self, segment, body):
-        lo, hi = (self.count * k // SEGMENTS for k in (segment, segment + 1))
-        lax.fori_loop(lo, hi, body, 0)
+    def row_cols(self, r):
+        if self.rows_n == 1:
+            return slice(0, SEQ_LEN)
+        return pl.ds(pl.multiple_of(r * SEQ_LEN, SEQ_LEN), SEQ_LEN)
+
+    def each_row(self, body):
+        if self.rows_n == 1:
+            body(0)
+        else:
+            lax.fori_loop(0, self.rows_n, lambda r, carry: (body(r), carry)[1], 0)
 
 
 def front_kernel(
@@ -471,7 +482,7 @@
     tok_ref, cot_ref, gain_ref, inw_ref, xw_ref, outw_ref, ch_ref, dtw_ref, resets_ref,
     x_out, act_out, step_out, dy_out, gated_out, dgate_out, pj_out, ng_out, cg_out, h0_out, dec_out, mask_out, ct_out,
     ng, cg, xs, gs, slope, acts, dgs, wxg, part, from_pair, pair, from_chips, pj,
-    mask, table, rowf, padded, step_ref, du_ref, y_ref, sums, wf, b8, c8, decb, h0, a_scr, gated, dgate,
+    mask, table, rowf, padded, step_ref, du_ref, y_ref, sums, wf, b8, c8, decb, h0, gated, dgate, inw, outw,
     ag_send, ag_recv, ag_rsend, ag_rrecv, ag_fsend, ag_frecv, rd_send, rd_recv, out_sem,
 ):
     here = Here(chan_size)
@@ -493,6 +504,10 @@
         pl.semaphore_signal(barrier, inc=1, device_id=(here.seq, here.same_core(k)), device_id_type=MESH)
     pl.semaphore_signal(barrier, inc=1, device_id=(here.seq, here.partner), device_id_type=MESH)
 
+    inner_load = pltpu.make_async_copy(inw_ref, inw, out_sem.at[out_sem.shape[0] - 1])
+    outer_load = pltpu.make_async_copy(outw_ref, outw, out_sem.at[out_sem.shape[0] - 2])
+    inner_load.start()
+    outer_load.start()
     order = reorder(own_rows).astype(bf16)
     values = tok_ref[...].astype(f32)
     normed = values * lax.rsqrt(jnp.mean(values * values, axis=-1, keepdims=True) + norm_epsilon) * gain_ref[...].reshape(1, width)
@@ -502,14 +517,18 @@
     )
     pl.semaphore_wait(barrier, chips)
     first = Gather(
-        here, ng, chips == 4, ag_send.at[0], ag_recv.at[0], ag_rsend.at[0], ag_rrecv.at[0], ag_fsend, ag_frecv
+        here, ng, chips == 4, *(sems.at[0] for sems in (ag_send, ag_recv, ag_rsend, ag_rrecv, ag_fsend, ag_frecv))
     )
-    second = Gather(here, cg, False, ag_send.at[1], ag_recv.at[1], ag_rsend.at[1], ag_rrecv.at[1], None, None)
+    second = Gather(
+        here, cg, False, *(sems.at[1] for sems in (ag_send, ag_recv, ag_rsend, ag_rrecv, ag_fsend, ag_frecv))
+    )
     first.start()
 
     cg[here.chan // per_row, :, here.chan % per_row] = dot_nn(order, cot_ref[...]).astype(bf16).reshape(shape)
-    wxg[0:channels, :] = inw_ref[0].astype(bf16)
-    wxg[channels:, :] = inw_ref[1].astype(bf16)
+    inner_load.wait()
+    outer_load.wait()
+    wxg[0:channels, :] = inw[0].astype(bf16)
+    wxg[channels:, :] = inw[1].astype(bf16)
     row_masks(resets_ref, mask)
     rowf[...] = jnp.zeros_like(rowf)
     rowf[0 : KC + 3, :] = ch_ref[0 : KC + 3, :]
@@ -587,9 +606,9 @@
 
     lax.fori_loop(0, channels // 16 * rows_n, gate_tile, 0)
     reduce.step3()
+    second.start()
     reduce.step4()
     reduce.step5()
-    second.start()
     save(pj, pj_out)
 
     padded[DT_COL : DT_COL + DR, :] = pj[0:DR, :]
@@ -606,7 +625,6 @@
             value = softplus(step_ref[rows, cols] + bias)
             step_ref[rows, cols] = value
             du_ref[rows, cols] = value * acts[rows, cols].astype(f32)
-            y_ref[rows, cols] = jnp.zeros((16, LANES), f32)
             total = total + jnp.where(mask[0:1, cols] > 0.0, HUGE, value)
         sums[pl.ds(pl.multiple_of(r * channels + i * 16, 16), 16), :] = total
         return carry
@@ -616,49 +634,56 @@
     save(step_ref, step_out)
     expand = expand_matrix()
 
-    def group(index, carry):
-        r, j, i, g = t.split(index)
-        rows = t.rows(i)
-        nrows = pl.ds(pl.multiple_of(g * (NG * 8), NG * 8), NG * 8)
-
-        @pl.when(j == 0)
-        def _():
-            if rows_n == 1:
-                block = pj[DR:, :]
-            else:
-                block = pj[DR:, pl.ds(pl.multiple_of(r * SEQ_LEN, SEQ_LEN), SEQ_LEN)]
-            b8[...] = dot_nn(expand, block[0:DS].astype(f32), highest)
-            c8[...] = dot_nn(expand, block[DS:].astype(f32), highest)
-
-        def tile(ref, s):
-            return ref[rows, t.cols(r, s)].reshape(1, CT, 8, LANES)
+    def scan_row(r):
+        block = pj[DR:, t.row_cols(r)]
+        b8[...] = dot_nn(expand, block[0:DS].astype(f32), highest)
+        c8[...] = dot_nn(expand, block[DS:].astype(f32), highest)
+
+        def tile(ref, rows, s):
+            return ref[rows, t.cols(r, s)].reshape(1, t.ct, 8, LANES)
 
         def state(ref, s):
-            return ref[nrows, slab(s)].reshape(NG, 1, 8, LANES)
-
-        dec = decb[pl.ds(g * NG, NG), rows, :].reshape(NG, CT, 8, LANES)
-        h = jnp.zeros((NG, CT, 8, LANES), f32)
-        for s in range(SLABS):
+            return ref[:, slab(s)].reshape(DS, 1, 8, LANES)
+
+        def keep(dec, rows, s):
             stepk = jnp.where(mask[0:1, t.cols(r, s)] > 0.0, HUGE, step_ref[rows, t.cols(r, s)])
-            a = jnp.exp2(dec * stepk.reshape(1, CT, 8, LANES))
-            a_scr[s] = a
-            h = a * h + state(b8, s) * tile(du_ref, s)
-        at = pl.ds(pl.multiple_of(r * channels + i * t.span, t.span), t.span)
-        for k in range(7):
-            gain = jnp.exp2(dec * wf[k, at, :].reshape(1, CT, 8, LANES))
-            h = h + gain * pltpu.roll(h, 1 << k, 3)
-        h = pltpu.roll(h, 1, 3)
-        h0[pl.ds(r * DS + g * NG, NG), rows, :] = h.reshape(NG, t.span, LANES)
-        for s in range(SLABS):
-            h = a_scr[s] * h + state(b8, s) * tile(du_ref, s)
-            y_ref[rows, t.cols(r, s)] += jnp.sum(state(c8, s) * h, axis=0).reshape(t.span, LANES)
-        return carry
-
-    for segment in range(SEGMENTS):
-        t.loop(segment, group)
-        if segment + 2 >= SEGMENTS:
-            for q in range(PIECES // 2):
-                second.pass_on(q + (segment + 2 - SEGMENTS) * PIECES // 2)
+            return jnp.exp2(dec * stepk.reshape(1, t.ct, 8, LANES))
+
+        of_row = pl.ds(r * DS, DS)
+
+        def chunk_ends(i, carry):
+            rows = t.rows(i)
+            dec = decb[:, rows, :].reshape(DS, t.ct, 8, LANES)
+            h = jnp.zeros((DS, t.ct, 8, LANES), f32)
+            for s in range(SLABS):
+                h = keep(dec, rows, s) * h + state(b8, s) * tile(du_ref, rows, s)
+            h0[of_row, rows, :] = h.reshape(DS, t.span, LANES)
+            return carry
+
+        def chunk_starts(i, carry):
+            rows = pl.ds(pl.multiple_of(i * high, high), high)
+            at = pl.ds(pl.multiple_of(r * channels + i * high, high), high)
+            h0[of_row, rows, :] = lane_scan(h0[of_row, rows, :], decb[:, rows, :], wf, at, False)
+            return carry
+
+        def outputs(i, carry):
+            rows = t.rows(i)
+            dec = decb[:, rows, :].reshape(DS, t.ct, 8, LANES)
+            h = h0[of_row, rows, :].reshape(DS, t.ct, 8, LANES)
+            for s in range(SLABS):
+                h = keep(dec, rows, s) * h + state(b8, s) * tile(du_ref, rows, s)
+                y_ref[rows, t.cols(r, s)] = jnp.sum(state(c8, s) * h, axis=0).reshape(t.span, LANES)
+            return carry
+
+        lax.fori_loop(0, t.tiles, chunk_ends, 0)
+        lax.fori_loop(0, channels // high, chunk_starts, 0)
+        if rows_n == 1:
+            second.pass_on(0)
+        lax.fori_loop(0, t.tiles, outputs, 0)
+
+    t.each_row(scan_row)
+    for q in range(1 if rows_n == 1 else 0, PIECES):
+        second.pass_on(q)
     save(h0, h0_out)
 
     def skip_tile(index, carry):
@@ -675,14 +700,14 @@
 
     lax.fori_loop(0, channels // 16 * rows_n, skip_tile, 0)
     save(gated, gated_out)
-    low = outw_ref[...].astype(bf16)
+    low = outw[...].astype(bf16)
     for q in range(PIECES):
         second.arrive(q)
+        save(cg.at[:, q * step : (q + 1) * step], cg_out.at[:, q * step : (q + 1) * step])
         for r in range(rows_n):
             block = cg[r, q * step : (q + 1) * step].reshape(span, width)
             cols = slice((r * PIECES + q) * span, (r * PIECES + q + 1) * span)
             dgs[:, cols] = dot_nt(low, block)
-    save(cg, cg_out)
 
     def grad_tile(index, carry):
         i = index // rows_n
@@ -732,18 +757,19 @@
         ((4, count), f32), ((channels, LANES), f32), ((LANES, channels), f32), ((LANES, count), bf16),
         (wide, f32), (wide, f32), (wide, f32), ((rows * channels, LANES), f32), ((7, rows * channels, LANES), f32),
         ((DS * 8, SEQ_LEN), f32), ((DS * 8, SEQ_LEN), f32), (decays, f32), (states, f32),
-        ((SLABS, NG, CT, 8, LANES), f32), (wide, bf16), (wide, bf16),
+        (wide, bf16), (wide, bf16),
+        ((2, channels, width), f32), ((channels, width), f32),
     ]
     return pl.pallas_call(
         functools.partial(front_kernel, chan_size),
-        in_specs=[vmem] * 9,
+        in_specs=[vmem] * 3 + [any_spec, vmem, any_spec] + [vmem] * 3,
         out_specs=[any_spec] * len(outs),
         out_shape=[jax.ShapeDtypeStruct(*o) for o in outs],
         scratch_shapes=[pltpu.VMEM(*s) for s in scratch]
         + [dma(gather_sems)] * 4
-        + [dma((PIECES,))] * 2
+        + [dma((2, PIECES))] * 2
         + [dma((2 * chips,))] * 2
-        + [dma((len(outs),))],
+        + [dma((len(outs) + PIECES + 2,))],
         compiler_params=pltpu.CompilerParams(collective_id=0, has_side_effects=True, vmem_limit_bytes=60 * MIB),
         name="front",
     )(tokens, cotangent, gain, in_weight, x_weight, out_weight, chan_params, dt_weight, resets)
@@ -753,11 +779,11 @@
     chan_size, seq_size,
     table, mask, xw_ref,
     gated_in, outw_in, cot_in, step_in, act_in, pj_in, dec_in, dy_in, h0_in, dgate_in, normed_in, inw_in, x_in,
-    msum_ref, dsum_ref, za_out, zb_out, zc_out, gsum_ref,
+    msum_ref, dsum_ref, za_out, zb_out, zc_out, zd_out, gsum_ref,
     gated, outw, step_ref, act, pjf, decb, dy, h0, dgate, inw, rows_buf, low, dx, dc, taps_red, gin1,
-    du, s1, ds2, totals, wb, b8, c8, db8, dc8, red, a_scr, ah_scr, pback,
-    part, pair_buf, land, from_pair, pair, from_chips, pj,
-    za, zb, zc, zha, zhb, zhc, gp, gz, gc,
+    du, s1, ds2, totals, wb, b8, c8, db8, dc8, red, p0, gate_part, a_scr, ah_scr, pback,
+    part, pair_buf, land, pair_d, land_d, from_pair, pair, from_chips, pj,
+    za, zb, zc, zd, zha, zhb, zhc, zhd, gp, gz, gc,
     in_sem, out_sem, m_s1, m_r1, m_s2, m_r2, d_s1, d_r1, d_s2, d_r2,
     rd_send, rd_recv, z_send, z_recv, gz_send, gz_recv, gc_send, gc_recv,
 ):
@@ -791,12 +817,14 @@
 
     reduce = Reduce(here, pback, from_pair, pair, from_chips, pj, rd_send, rd_recv)
     mixed = Scatter(here, part, pair_buf, land, m_s1, m_r1, m_s2, m_r2)
-    normed_grad = Scatter(here, part, pair_buf, land, d_s1, d_r1, d_s2, d_r2)
+    own = (pair_d, land_d) if rows_n == 1 else (pair_buf, land)
+    normed_grad = Scatter(here, part, *own, d_s1, d_r1, d_s2, d_r2)
     sum_a = SeqSum(here, seq_size, za, zha, z_send.at[0], z_recv.at[0])
     sum_b = SeqSum(here, seq_size, zb, zhb, z_send.at[1], z_recv.at[1])
     sum_c = SeqSum(here, seq_size, zc, zhc, z_send.at[2], z_recv.at[2])
+    sum_d = SeqSum(here, seq_size, zd, zhd, z_send.at[3], z_recv.at[3])
     if za.shape[0] > channels:
-        for buf in (za, zb, zc):
+        for buf in (za, zb, zc, zd):
             buf[channels:, :] = jnp.zeros((buf.shape[0] - channels, buf.shape[1]), bf16)
 
     def row_block(slot):
@@ -818,7 +846,8 @@
             loads[name].start()
     low[0] = outw[...].astype(bf16)
     pl.semaphore_wait(barrier, chan_size - 1 + seq_size - 1)
-    mixed.produce(lambda cols: dot_tn(gated[:, cols], low[0]), False, None)
+    mixed.produce(lambda cols: dot_tn(gated[:, cols], low[0]), True, lambda: None)
+    mixed.send(PIECES - 1)
     loads["cot"].wait()
     out_grad = dot_nn(gated[:, row_cols(0)], row_block(0))
     for r in range(1, rows_n):
@@ -860,79 +889,93 @@
 
     lax.fori_loop(0, tile_count, prelude, 0)
     windows(totals, wb, True)
-    for q in range(PIECES):
-        mixed.send(q)
     expand = expand_matrix()
 
-    def group(index, carry):
-        r, j, i, g = t.split(index)
-        rows = t.rows(i)
-        nrows = pl.ds(pl.multiple_of(g * (NG * 8), NG * 8), NG * 8)
-        whole_row = slice(0, SEQ_LEN) if rows_n == 1 else pl.ds(pl.multiple_of(r * SEQ_LEN, SEQ_LEN), SEQ_LEN)
-
-        @pl.when(j == 0)
-        def _():
-            block = pjf[DR:, whole_row]
-            b8[...] = dot_nn(expand, block[0:DS].astype(f32), highest)
-            c8[...] = dot_nn(expand, block[DS:].astype(f32), highest)
-            db8[...] = jnp.zeros_like(db8)
-            dc8[...] = jnp.zeros_like(dc8)
-
-        def tile(ref, s):
-            return ref[rows, t.cols(r, s)].reshape(1, CT, 8, LANES)
+    high = tall(channels)
+    levels = seq_size.bit_length() - 1
+
+    def adjoint_row(r):
+        whole_row = t.row_cols(r)
+        block = pjf[DR:, whole_row]
+        b8[...] = dot_nn(expand, block[0:DS].astype(f32), highest)
+        c8[...] = dot_nn(expand, block[DS:].astype(f32), highest)
+        db8[...] = jnp.zeros_like(db8)
+        dc8[...] = jnp.zeros_like(dc8)
+
+        def tile(ref, rows, s):
+            return ref[rows, t.cols(r, s)].reshape(1, t.ct, 8, LANES)
 
         def state(ref, s):
-            return ref[nrows, slab(s)].reshape(NG, 1, 8, LANES)
-
-        dec = decb[pl.ds(g * NG, NG), rows, :].reshape(NG, CT, 8, LANES)
-        h = h0[pl.ds(r * DS + g * NG, NG), rows, :].reshape(NG, CT, 8, LANES)
-        for s in range(SLABS):
+            return ref[:, slab(s)].reshape(DS, 1, 8, LANES)
+
+        def keep(dec, rows, s):
             stepk = jnp.where(mask[0:1, t.cols(r, s)] > 0.0, HUGE, step_ref[rows, t.cols(r, s)])
-            a = jnp.exp2(dec * stepk.reshape(1, CT, 8, LANES))
-            a_scr[s] = a
-            ah = a * h
-            ah_scr[s] = ah
-            h = ah + state(b8, s) * tile(du, s)
-            dc8[nrows, slab(s)] += jnp.sum(tile(dy, s) * h, axis=1).reshape(NG * 8, LANES)
-        p = jnp.zeros((NG, CT, 8, LANES), f32)
-        for s in reversed(range(SLABS)):
-            p = a_scr[s] * (tile(dy, s) * state(c8, s) + p)
-        at = pl.ds(pl.multiple_of(r * channels + i * t.span, t.span), t.span)
-        for k in range(7):
-            gain = jnp.exp2(dec * wb[k, at, :].reshape(1, CT, 8, LANES))
-            p = p + gain * pltpu.roll(p, LANES - (1 << k), 3)
-        p = pltpu.roll(p, LANES - 1, 3)
-        rate = jnp.zeros((NG, CT, 8, LANES), f32)
-        for s in reversed(range(SLABS)):
-            lam = tile(dy, s) * state(c8, s) + p
-            p = a_scr[s] * lam
-            s1[rows, t.cols(r, s)] += jnp.sum(lam * state(b8, s), axis=0).reshape(t.span, LANES)
-            db8[nrows, slab(s)] += jnp.sum(lam * tile(du, s), axis=1).reshape(NG * 8, LANES)
-            q = lam * ah_scr[s]
-            ds2[rows, t.cols(r, s)] += jnp.sum(dec * q, axis=0).reshape(t.span, LANES)
-            rate = rate + q * tile(step_ref, s)
-        for n in range(NG):
-            cols = pl.ds(pl.multiple_of((g * NG + n) * LANES, LANES), LANES)
-            red[rows, cols] += rate[n].reshape(t.span, LANES)
-
-        @pl.when(j == t.per_row - 1)
-        def _():
-            pback[DR : DR + DS, whole_row] = dot_tn(expand, db8[...], highest).astype(bf16)
-            pback[DR + DS :, whole_row] = dot_tn(expand, dc8[...], highest).astype(bf16)
-
-        return carry
-
-    levels = seq_size.bit_length() - 1
-    for segment in range(SEGMENTS):
-        t.loop(segment, group)
-        if segment == 1:
+            return jnp.exp2(dec * stepk.reshape(1, t.ct, 8, LANES))
+
+        def chunk_ends(i, carry):
+            rows = t.rows(i)
+            dec = decb[:, rows, :].reshape(DS, t.ct, 8, LANES)
+            p = jnp.zeros((DS, t.ct, 8, LANES), f32)
+            for s in reversed(range(SLABS)):
+                p = keep(dec, rows, s) * (tile(dy, rows, s) * state(c8, s) + p)
+            p0[:, rows, :] = p.reshape(DS, t.span, LANES)
+            return carry
+
+        def chunk_starts(i, carry):
+            rows = pl.ds(pl.multiple_of(i * high, high), high)
+            at = pl.ds(pl.multiple_of(r * channels + i * high, high), high)
+            p0[:, rows, :] = lane_scan(p0[:, rows, :], decb[:, rows, :], wb, at, True)
+            return carry
+
+        def adjoints(index, carry):
+            i, g = index // (DS // NG), index % (DS // NG)
+            rows = t.rows(i)
+            some = pl.ds(g * NG, NG)
+            lines = pl.ds(pl.multiple_of(g * (NG * 8), NG * 8), NG * 8)
+            shape = (NG, t.ct, 8, LANES)
+
+            def state(ref, s):
+                return ref[lines, slab(s)].reshape(NG, 1, 8, LANES)
+
+            dec = decb[some, rows, :].reshape(shape)
+            h = h0[pl.ds(r * DS + g * NG, NG), rows, :].reshape(shape)
+            for s in range(SLABS):
+                a = keep(dec, rows, s)
+                a_scr[s] = a
+                ah = a * h
+                ah_scr[s] = ah
+                h = ah + state(b8, s) * tile(du, rows, s)
+                dc8[lines, slab(s)] += jnp.sum(tile(dy, rows, s) * h, axis=1).reshape(NG * 8, LANES)
+            p = p0[some, rows, :].reshape(shape)
+            rate = jnp.zeros(shape, f32)
+            for s in reversed(range(SLABS)):
+                lam = tile(dy, rows, s) * state(c8, s) + p
+                p = a_scr[s] * lam
+                s1[rows, t.cols(r, s)] += jnp.sum(lam * state(b8, s), axis=0).reshape(t.span, LANES)
+                db8[lines, slab(s)] += jnp.sum(lam * tile(du, rows, s), axis=1).reshape(NG * 8, LANES)
+                q = lam * ah_scr[s]
+                ds2[rows, t.cols(r, s)] += jnp.sum(dec * q, axis=0).reshape(t.span, LANES)
+                rate = rate + q * tile(step_ref, rows, s)
+            for n in range(NG):
+                cols = pl.ds(pl.multiple_of((g * NG + n) * LANES, LANES), LANES)
+                red[rows, cols] += rate[n].reshape(t.span, LANES)
+            return carry
+
+        lax.fori_loop(0, t.tiles, chunk_ends, 0)
+        lax.fori_loop(0, channels // high, chunk_starts, 0)
+        if rows_n == 1:
             sum_a.step(0)
             sum_b.step(0)
-        if segment + 1 == SEGMENTS:
-            for i in range(1, levels):
-                sum_a.step(i)
-                sum_b.step(i)
-            mixed.finish(msum_ref)
+        lax.fori_loop(0, t.tiles * (DS // NG), adjoints, 0)
+        pback[DR : DR + DS, whole_row] = dot_tn(expand, db8[...], highest).astype(bf16)
+        pback[DR + DS :, whole_row] = dot_tn(expand, dc8[...], highest).astype(bf16)
+
+    t.each_row(adjoint_row)
+    if rows_n > 1:
+        sum_a.step(0)
+        sum_b.step(0)
+    if rows_n > 1:
+        mixed.finish(msum_ref)
     loads["x"].start()
     x_buf = du
 
@@ -974,19 +1017,24 @@
         ],
         axis=1,
     )
-    zc[0:channels, width + LANES :] = (dot_nn(red[...], pick, highest) + dt_grad).astype(bf16)
+    zd[0:channels, :] = (dot_nn(red[...], pick, highest) + dt_grad).astype(bf16)
+    sum_d.start()
     reduce.step2()
     reduce.step3()
+    if rows_n == 1:
+        for q in range(PIECES):
+            cols = slice(q * SEQ_LEN // PIECES, (q + 1) * SEQ_LEN // PIECES)
+            gate_part[cols, :] = dot_tn(dgate[:, cols], low[1])
     reduce.step4()
-    saves = sum_a.finish(za_out, out_sem.at[0])
-    saves += sum_b.finish(zb_out, out_sem.at[1])
+    for i in range(1, levels):
+        sum_a.step(i)
+        sum_b.step(i)
+    sum_d.step(0)
     loads["x"].wait()
     x_low = xw_ref[...].astype(bf16)
     reduce.step5()
     for r in range(rows_n):
         s1[:, row_cols(r)] += dot_tn(x_low, pj[:, row_cols(r)])
-
-    high = tall(channels)
 
     def conv_tile(index, carry):
         i = index // rows_n
@@ -1054,9 +1102,12 @@
         both = low[0].astype(f32) * in_grad + low[1].astype(f32) * gin1[...]
         gp[...] = jnp.sum(both.reshape(channels // 8, 8, width), axis=0)
 
-    normed_grad.produce(
-        lambda cols: dot_tn(dx[:, cols], low[0]) + dot_tn(dgate[:, cols], low[1]), True, weight_sums
-    )
+    def normed_part(cols):
+        gate = gate_part[cols, :] if rows_n == 1 else dot_tn(dgate[:, cols], low[1])
+        return dot_tn(dx[:, cols], low[0]) + gate
+
+    weight_sums()
+    normed_grad.produce(normed_part, True, lambda: None)
     normed_grad.send(PIECES - 1)
 
     def gain_seq(k):
@@ -1078,8 +1129,15 @@
     gz[seq_size - 1] = total
     for k in range(1, chan_size):
         gain_chan(k).start()
+    saves = sum_a.finish(za_out, out_sem.at[0])
+    saves += sum_b.finish(zb_out, out_sem.at[1])
+    for i in range(1, levels):
+        sum_d.step(i)
+    if rows_n == 1:
+        mixed.finish(msum_ref)
     for i in range(levels):
         sum_c.step(i)
+    saves += sum_d.finish(zd_out, out_sem.at[3])
     for k in range(1, chan_size):
         gain_chan(k).wait()
         total = total + gc[k - 1]
@@ -1108,12 +1166,12 @@
     any_spec = pl.BlockSpec(memory_space=pl.ANY)
     vmem = pl.BlockSpec(memory_space=pltpu.VMEM)
     dma = pltpu.SemaphoreType.DMA
-    sums = ((padded, width), (padded, width), (padded, width + 2 * LANES))
+    sums = ((padded, width), (padded, width), (padded, width + LANES), (padded, LANES))
     states = (DS * 8, SEQ_LEN)
-    loops = (SLABS, NG, CT, 8, LANES)
+    loops = (SLABS, NG, tile_depth(rows), 8, LANES)
     outs = [
         ((own_rows, width), f32), ((own_rows, width), f32), (sums[0], bf16), (sums[1], bf16), (sums[2], bf16),
-        ((8, width), f32),
+        (sums[3], bf16), ((8, width), f32),
     ]
     scratch = [
         (wide, bf16), ((channels, width), f32), (wide, f32), (wide, bf16), ((project, count), bf16),
@@ -1123,24 +1181,27 @@
         ((channels, width), f32),
         (wide, f32), (wide, f32), (wide, f32), ((rows * channels, LANES), f32), ((7, rows * channels, LANES), f32),
         (states, f32), (states, f32), (states, f32), (states, f32), ((channels, (DS + 2) * LANES), f32),
-        (loops, f32), (loops, f32), ((project, count), bf16),
+        ((DS, channels, LANES), f32), ((SEQ_LEN if rows == 1 else 8, width), f32), (loops, f32), (loops, f32), ((project, count), bf16),
         ((min(rows, 2), SLABS, per_row, 2, lanes, width), bf16), ((rows, SLABS, per_row, lanes, width), bf16),
-        ((chips - 1, SLABS, lanes, width), bf16), ((project, count // 2), bf16), ((project, count // 2), bf16),
+        ((chips - 1, SLABS, lanes, width), bf16),
+        ((rows, SLABS, per_row, lanes, width) if rows == 1 else (16, LANES), bf16),
+        ((chips - 1, SLABS, lanes, width) if rows == 1 else (16, LANES), bf16),
+        ((project, count // 2), bf16), ((project, count // 2), bf16),
         ((chips - 1, project, count // 2 // chips), bf16), ((project, count), bf16),
-        (sums[0], bf16), (sums[1], bf16), (sums[2], bf16),
+        (sums[0], bf16), (sums[1], bf16), (sums[2], bf16), (sums[3], bf16),
     ]
     scratch += [((levels + 1, padded // 2, s[1]), bf16) for s in sums]
     scratch += [((8, width), f32), ((seq_size, 8, width), f32), ((chan_size - 1, 8, width), f32)]
     return pl.pallas_call(
         functools.partial(back_kernel, chan_size, seq_size),
         in_specs=[vmem] * 3 + [any_spec] * 13,
-        out_specs=[vmem, vmem, any_spec, any_spec, any_spec, vmem],
+        out_specs=[vmem, vmem, any_spec, any_spec, any_spec, any_spec, vmem],
         out_shape=[jax.ShapeDtypeStruct(*o) for o in outs],
         scratch_shapes=[pltpu.VMEM(*s) for s in scratch]
-        + [dma((13,)), dma((3, 2))]
+        + [dma((13,)), dma((4, 2))]
         + ([dma((rows * PIECES,))] * 2 + [dma((chips * PIECES,))] * 2) * 2
         + [dma((2 * chips,))] * 2
-        + [dma((3, levels + 1))] * 2
+        + [dma((4, levels + 1))] * 2
         + [dma((seq_size,))] * 2
         + [dma((chan_size,))] * 2,
         compiler_params=pltpu.CompilerParams(collective_id=1, has_side_effects=True, vmem_limit_bytes=60 * MIB),
@@ -1217,7 +1278,7 @@
             ref[...] = value.reshape(width)
 
 
-def finish_call(tokens, cotangent, msum, dsum, za, zb, zc, gsum, gains, inners, projects, steps, outputs, chans):
+def finish_call(tokens, cotangent, msum, dsum, za, zb, zc, zd, gsum, gains, inners, projects, steps, outputs, chans):
     own_rows, width = tokens.shape
     channels = outputs[0].shape[0]
     cb = 96 if channels % 96 == 0 else channels
@@ -1230,14 +1291,14 @@
 
     inner = pl.BlockSpec((2, cb, width), lambda i: (0, i, 0))
     outer = pl.BlockSpec((cb, width), lambda i: (i, 0))
-    tails = [pl.BlockSpec((zc.shape[0], LANES), lambda i, k=k: (0, width // LANES + k)) for k in (1, 0)]
+    tails = [full(zd.shape), pl.BlockSpec((zc.shape[0], LANES), lambda i: (0, width // LANES))]
     zed = pl.BlockSpec((cb, width), lambda i: (i, 0))
     groups = (gains, inners, projects, steps, outputs, chans)
     specs = (full(gains[0].shape), inner, full(projects[0].shape), full(steps[0].shape), outer, full(chans[0].shape))
     in_specs = [row, row, full(msum.shape), full(dsum.shape), zed, zed, zed, *tails, full(gsum.shape)]
     out_specs = [row, row]
     out_shape = [jax.ShapeDtypeStruct(tokens.shape, bf16), jax.ShapeDtypeStruct(tokens.shape, f32)]
-    args = [tokens, cotangent, msum, dsum, za, zb, zc, zc, zc, gsum]
+    args = [tokens, cotangent, msum, dsum, za, zb, zc, zd, zc, gsum]
     for arrays, spec in zip(groups, specs):
         in_specs += [spec] * 3
         out_specs += [spec] * 4
@@ -1287,12 +1348,12 @@
         chan_size, tokens, cotangent, norm_gain, inners[0], projects[0], out_weight, chan_params, dt_weight,
         resets.reshape(-1, LANES),
     )
-    msum, dsum, za, zb, zc, gsum = back_call(
+    msum, dsum, za, zb, zc, zd, gsum = back_call(
         chan_size, seq_size, own_count, table, masks, projects[0], gated, out_weight, cot_all, step, act, pj, decays, dy, h0,
         dgate, normed_all, inners[0], x_cols,
     )
     result = finish_call(
-        tokens, cotangent, msum, dsum, za, zb, zc, gsum,
+        tokens, cotangent, msum, dsum, za, zb, zc, zd, gsum,
         (norm_gain, gain_first, gain_second),
         inners,
         projects,

time: 163 us -> 158 us (0.969); the launches traced: 160 us -> 157 us
  Pallas kernels: 159 us -> 156 us
where the time goes in v1:
time: 158 us; the launch traced here: 157 us
  Pallas kernels  156 us (99%)
    pallas_call x1, Pallas kernels, back_call(): pl.pallas_call(functools.partial(back_kernel, chan_size, seq_size), in_sp...  87.1 us
    pallas_call x1, Pallas kernels, front_call(): pl.pallas_call(functools.partial(front_kernel, chan_size), in_specs=[vmem...  60.5 us
    pallas_call x1, Pallas kernels, finish_call(): pl.pallas_call(finish_kernel, grid=(grid,), in_specs=in_specs, out_specs=...  8.9 us

profile of v1, /device:TPU:0, one launch (start us, length us, event | category | flops | bytes accessed | tf_op | source)
XLA Modules:
  0.0 157.4 jit_solution(3839944811421590295)
XLA Ops:
  0.7 60.5 %front.1 = (f32[192,2048]{1,0:T(8,128)}, bf16[192,2048]{1,0:T(8,128)(2,1)}, f32[192,2048]{1,0:T(8,128)}, f32[192,2048]{1,0:T(8,128)}, bf16[192,2048]{1,0:T(8,128...) custom-call(bf16[256,768]{1,0:T(8,128)(2,1)} %tok_ref.3, ...), custom_call_target="tpu_custom_call" | custom-call | tf_op jit(solution)/shard_map/front/pallas_call | solution.py:763
  61.2 87.1 %back.1 = (f32[256,768]{1,0:T(8,128)}, f32[256,768]{1,0:T(8,128)}, bf16[192,768]{1,0:T(8,128)(2,1)}, bf16[192,768]{1,0:T(8,128)(2,1)}, bf16[192,896]{1,0:T(8,128...) custom-call(f32[192,128]{1,0:T(8,128)} %get-tuple-element.72.table, f32[4,2048]{1,0:T(4,128)} %get-tuple-element.73.mask, ...), custom_call_target="tpu_custom_call" | custom-call | tf_op jit(solution)/shard_map/back/pallas_call | solution.py:1195
  148.3 8.9 %finish.1 = (bf16[256,768]{1,0:T(8,128)(2,1)}, f32[256,768]{1,0:T(8,128)}, f32[768]{0:T(1024)}, f32[768]{0:T(1024)}, f32[768]{0:T(1024)}, /*index=5*/bf16[768]{0...) custom-call(bf16[256,768]{1,0:T(8,128)(2,1)} %tok_ref.3, ...), custom_call_target="tpu_custom_call" | custom-call | tf_op jit(solution)/shard_map/finish/pallas_call | solution.py:1307
